TPU v7x, 32 devices: a whole 2x2x4 slice. The times are simulated.
32 devices in a mesh: ctx: 16 (over z, y, core), fsdp: 2 (over x).
Axes of the slice: x: 2, y: 2, z: 4, core: 2. Of those that a mesh axis runs over, the one named last changes fastest.
Arguments:
- tokens: bfloat16 [2, 4096, 768], P('fsdp', 'ctx')
- segments: int32 [2, 4096], P('fsdp', 'ctx'), may hold values from 0 to 6, as said below
- cotangent: bfloat16 [2, 4096, 768], P('fsdp', 'ctx'), may hold values from -6 to 6
- ln1_gain: bfloat16 [768], P('fsdp'), may hold values from 0.5 to 1.5
- ln1_bias: bfloat16 [768], P('fsdp'), may hold values from -4 to 4
- qkv_weight: bfloat16 [768, 2304], P('fsdp'), may hold values from -0.21875 to 0.21875
- q_bias: bfloat16 [768], P('fsdp'), may hold values from -4 to 4
- v_bias: bfloat16 [768], P('fsdp'), may hold values from -4 to 4
- out_weight: bfloat16 [768, 768], P('fsdp'), may hold values from -0.21875 to 0.21875
- out_bias: bfloat16 [768], P('fsdp'), may hold values from -4 to 4
- ln2_gain: bfloat16 [768], P('fsdp'), may hold values from 0.5 to 1.5
- ln2_bias: bfloat16 [768], P('fsdp'), may hold values from -4 to 4
- up_weight: bfloat16 [768, 3072], P('fsdp')
- up_bias: bfloat16 [3072], P('fsdp'), may hold values from -4 to 4
- down_weight: bfloat16 [3072, 768], P('fsdp'), may hold values from -0.109375 to 0.109375
- down_bias: bfloat16 [768], P('fsdp'), may hold values from -4 to 4
Outputs:
- layer_out: bfloat16 [2, 4096, 768], P('fsdp', 'ctx')
- input_grad: bfloat16 [2, 4096, 768], P('fsdp', 'ctx')
- ln1_gain_grad: float32 [768], P('fsdp')
- ln1_bias_grad: float32 [768], P('fsdp')
- qkv_weight_grad: float32 [768, 2304], P('fsdp')
- q_bias_grad: float32 [768], P('fsdp')
- v_bias_grad: float32 [768], P('fsdp')
- out_weight_grad: float32 [768, 768], P('fsdp')
- out_bias_grad: float32 [768], P('fsdp')
- ln2_gain_grad: float32 [768], P('fsdp')
- ln2_bias_grad: float32 [768], P('fsdp')
- up_weight_grad: float32 [768, 3072], P('fsdp')
- up_bias_grad: float32 [3072], P('fsdp')
- down_weight_grad: float32 [3072, 768], P('fsdp')
- down_bias_grad: float32 [768], P('fsdp')
- stream_rms: float32 [3], replicated
Inputs may be any that keep to these rules, and one draw needn't show every extreme that they name: `segments`: the nonzero segment numbers never fall along a sequence; runs of padding (0) may stand between or inside documents and at a sequence's end. One document of each sequence has tokens within its first 256 tokens and within its last 256.
All inputs are finite; a program needn't handle non-finite values.
Results may differ from a plain program's by a relative error of at most 0.019.
Values may be sent and summed in bfloat16 or wider, within the bound.
No kernel may reach another device: no remote copies, remote signals or barrier semaphores. Data moves between devices by JAX's collectives and lax.ppermute only.
A program may use at most 128 MiB of HBM per device.

v0:
```python
import jax
import jax.numpy as jnp
from jax import lax
from jax.sharding import PartitionSpec as P

HEADS = 12
HEAD_DIM = 64


EPS = 1e-06
NEG = -1000000000.0


def shifted(block, axis, distance):
    devices = range(lax.axis_size(axis))
    route = [((i - distance) % len(devices), i) for i in devices]
    return lax.ppermute(block, axis, route)


def layer_norm(inputs, gain_vec, bias_vec):
    row_mean = jnp.mean(inputs, axis=-1, keepdims=True)
    centred = inputs - row_mean
    variance = jnp.mean(centred * centred, axis=-1, keepdims=True)
    return centred * lax.rsqrt(variance + EPS) * gain_vec + bias_vec


def gelu_tanh(inputs):
    return jax.nn.gelu(inputs, approximate=True)


def rows_product(left, right):
    return lax.dot_general(
        left, right, (((0,), (0,)), ((), ())), preferred_element_type=jnp.float32
    )


def cols_product(left, right):
    return lax.dot_general(
        left, right, (((1,), (1,)), ((), ())), preferred_element_type=jnp.float32
    )


def body(
    tokens,
    segments,
    cotangent,
    ln1_gain,
    ln1_bias,
    qkv_weight,
    q_bias,
    v_bias,
    out_weight,
    out_bias,
    ln2_gain,
    ln2_bias,
    up_weight,
    up_bias,
    down_weight,
    down_bias,
):
    tok_rows = tokens.shape[1]
    model_width = tokens.shape[2]
    score_scale = HEAD_DIM ** (-0.5)
    cycle_size = lax.axis_size("ctx")
    cycle_index = lax.axis_index("ctx")
    gain_one, shift_one, w_qkv, bias_query, bias_value, w_out, bias_out = (
        lax.all_gather(ln1_gain, "fsdp", axis=0, tiled=True),
        lax.all_gather(ln1_bias, "fsdp", axis=0, tiled=True),
        lax.all_gather(qkv_weight, "fsdp", axis=0, tiled=True),
        lax.all_gather(q_bias, "fsdp", axis=0, tiled=True),
        lax.all_gather(v_bias, "fsdp", axis=0, tiled=True),
        lax.all_gather(out_weight, "fsdp", axis=0, tiled=True),
        lax.all_gather(out_bias, "fsdp", axis=0, tiled=True),
    )
    gain_one = gain_one.astype(jnp.float32)
    shift_one = shift_one.astype(jnp.float32)
    bias_query = bias_query.astype(jnp.float32)
    bias_value = bias_value.astype(jnp.float32)
    bias_out = bias_out.astype(jnp.float32)
    all_seg = lax.all_gather(segments, "ctx", axis=1, tiled=True)[0]
    own_seg = segments[0]
    layer_in = tokens[0].astype(jnp.float32)
    normed = layer_norm(layer_in, gain_one, shift_one).astype(jnp.bfloat16)
    qkv_bias = jnp.concatenate([bias_query, jnp.zeros_like(bias_query), bias_value])
    qkv = (jnp.dot(normed, w_qkv, preferred_element_type=jnp.float32) + qkv_bias).astype(
        jnp.bfloat16
    )
    queries = qkv[:, :model_width].reshape(tok_rows, HEADS, HEAD_DIM)
    keys = qkv[:, model_width : 2 * model_width]
    values = qkv[:, 2 * model_width :]

    def attend(state_now, key_block, value_block, key_seg):
        run_max, run_sum, run_out = state_now
        key_heads = key_block.reshape(-1, HEADS, HEAD_DIM)
        value_heads = value_block.reshape(-1, HEADS, HEAD_DIM)
        scores = (
            jnp.einsum("qhd,khd->hqk", queries, key_heads, preferred_element_type=jnp.float32)
            * score_scale
        )
        same_doc = (own_seg[:, None] == key_seg[None, :])[None]
        new_max = jnp.maximum(run_max, jnp.max(jnp.where(same_doc, scores, NEG), axis=-1))
        weights = jnp.where(same_doc, jnp.exp(scores - new_max[..., None]), 0.0)
        fading = jnp.exp(run_max - new_max)
        run_sum = run_sum * fading + jnp.sum(weights, axis=-1)
        run_out = run_out * fading[..., None] + jnp.einsum(
            "hqk,khd->hqd",
            weights.astype(jnp.bfloat16),
            value_heads,
            preferred_element_type=jnp.float32,
        )
        return (new_max, run_sum, run_out)

    def attend_step(state_now, member):
        return (attend(state_now, member[0], member[1], member[2]), None)

    start_state = (
        jnp.full((HEADS, tok_rows), NEG, jnp.float32),
        jnp.zeros((HEADS, tok_rows), jnp.float32),
        jnp.zeros((HEADS, tok_rows, HEAD_DIM), jnp.float32),
    )
    state_now = start_state
    key_piece = lax.all_gather(keys, "ctx", axis=0, tiled=True)
    value_piece = lax.all_gather(values, "ctx", axis=0, tiled=True)
    blocks = key_piece.shape[0] // tok_rows
    key_seg = all_seg
    state_now, _ = lax.scan(
        attend_step,
        state_now,
        (
            key_piece.reshape(blocks, tok_rows, model_width),
            value_piece.reshape(blocks, tok_rows, model_width),
            key_seg.reshape(blocks, tok_rows),
        ),
    )
    run_max, run_sum, run_out = state_now
    log_total = run_max + jnp.log(run_sum)
    attn_f = (run_out / run_sum[..., None]).transpose(1, 0, 2).reshape(tok_rows, model_width)
    attn_low = attn_f.astype(jnp.bfloat16)
    gain_two, shift_two, w_up, bias_up, w_down, bias_down = (
        lax.all_gather(ln2_gain, "fsdp", axis=0, tiled=True),
        lax.all_gather(ln2_bias, "fsdp", axis=0, tiled=True),
        lax.all_gather(up_weight, "fsdp", axis=0, tiled=True),
        lax.all_gather(up_bias, "fsdp", axis=0, tiled=True),
        lax.all_gather(down_weight, "fsdp", axis=0, tiled=True),
        lax.all_gather(down_bias, "fsdp", axis=0, tiled=True),
    )
    gain_two = gain_two.astype(jnp.float32)
    shift_two = shift_two.astype(jnp.float32)
    bias_up = bias_up.astype(jnp.float32)
    bias_down = bias_down.astype(jnp.float32)
    mid_stream = layer_in + jnp.dot(attn_low, w_out, preferred_element_type=jnp.float32) + bias_out
    normed_two = layer_norm(mid_stream, gain_two, shift_two).astype(jnp.bfloat16)
    up_pre = jnp.dot(normed_two, w_up, preferred_element_type=jnp.float32) + bias_up
    hidden_f, gelu_back = jax.vjp(gelu_tanh, up_pre)
    hidden = hidden_f.astype(jnp.bfloat16)
    out_stream = (
        mid_stream + jnp.dot(hidden, w_down, preferred_element_type=jnp.float32) + bias_down
    )
    valid = (own_seg > 0).astype(jnp.float32)[:, None]
    squares = jnp.stack(
        [
            jnp.sum(valid * layer_in * layer_in),
            jnp.sum(valid * mid_stream * mid_stream),
            jnp.sum(valid * out_stream * out_stream),
        ]
    )
    counted = jnp.sum(valid)
    square_sums, count_sum = lax.psum((squares, counted), ("ctx", "fsdp"))
    stream_rms = jnp.sqrt(square_sums / (count_sum * model_width))
    grad_out = cotangent[0]
    grad_stream = grad_out.astype(jnp.float32)
    d_down_bias = jnp.sum(grad_stream, axis=0)
    d_down_weight = rows_product(hidden, grad_out)
    d_hidden = cols_product(grad_out, w_down)
    d_up = gelu_back(d_hidden)[0]
    d_up_bias = jnp.sum(d_up, axis=0)
    d_up_low = d_up.astype(jnp.bfloat16)
    d_up_weight = rows_product(normed_two, d_up_low)
    d_normed_two = cols_product(d_up_low, w_up)
    _, norm_two_back = jax.vjp(layer_norm, mid_stream, gain_two, shift_two)
    d_mid_norm, d_gain_two, d_shift_two = norm_two_back(d_normed_two)
    d_mid = grad_stream + d_mid_norm
    mlp_shards = (
        lax.psum_scatter(
            d_gain_two.astype(jnp.bfloat16), "fsdp", scatter_dimension=0, tiled=True
        ).astype(jnp.float32),
        lax.psum_scatter(
            d_shift_two.astype(jnp.bfloat16), "fsdp", scatter_dimension=0, tiled=True
        ).astype(jnp.float32),
        lax.psum_scatter(
            d_up_weight.astype(jnp.bfloat16), "fsdp", scatter_dimension=0, tiled=True
        ).astype(jnp.float32),
        lax.psum_scatter(
            d_up_bias.astype(jnp.bfloat16), "fsdp", scatter_dimension=0, tiled=True
        ).astype(jnp.float32),
        lax.psum_scatter(
            d_down_weight.astype(jnp.bfloat16), "fsdp", scatter_dimension=0, tiled=True
        ).astype(jnp.float32),
        lax.psum_scatter(
            d_down_bias.astype(jnp.bfloat16), "fsdp", scatter_dimension=0, tiled=True
        ).astype(jnp.float32),
    )
    d_out_bias = jnp.sum(d_mid, axis=0)
    d_mid_low = d_mid.astype(jnp.bfloat16)
    d_out_weight = rows_product(attn_low, d_mid_low)
    d_attn_low = cols_product(d_mid_low, w_out).astype(jnp.bfloat16)
    d_heads = d_attn_low.reshape(tok_rows, HEADS, HEAD_DIM)
    delta = jnp.sum(
        d_attn_low.astype(jnp.float32).reshape(tok_rows, HEADS, HEAD_DIM)
        * attn_f.reshape(tok_rows, HEADS, HEAD_DIM),
        axis=-1,
    ).T

    def grad_block(grad_query, key_block, value_block, key_seg):
        key_heads = key_block.reshape(-1, HEADS, HEAD_DIM)
        value_heads = value_block.reshape(-1, HEADS, HEAD_DIM)
        scores = (
            jnp.einsum("qhd,khd->hqk", queries, key_heads, preferred_element_type=jnp.float32)
            * score_scale
        )
        same_doc = (own_seg[:, None] == key_seg[None, :])[None]
        probs = jnp.where(same_doc, jnp.exp(scores - log_total[..., None]), 0.0)
        d_probs = jnp.einsum(
            "qhd,khd->hqk", d_heads, value_heads, preferred_element_type=jnp.float32
        )
        d_scores = (probs * (d_probs - delta[..., None])).astype(jnp.bfloat16)
        grad_query = (
            grad_query
            + jnp.einsum("hqk,khd->qhd", d_scores, key_heads, preferred_element_type=jnp.float32)
            * score_scale
        )
        key_part = (
            jnp.einsum("hqk,qhd->khd", d_scores, queries, preferred_element_type=jnp.float32)
            * score_scale
        )
        value_part = jnp.einsum(
            "hqk,qhd->khd", probs.astype(jnp.bfloat16), d_heads, preferred_element_type=jnp.float32
        )
        return (grad_query, key_part.reshape(-1, model_width), value_part.reshape(-1, model_width))

    query_start = jnp.zeros((tok_rows, HEADS, HEAD_DIM), jnp.float32)

    def rotate_keys(key_block, value_block):
        return shifted((key_block, value_block), "ctx", 1)

    def rotate_grads(grad_key, grad_value):
        return (
            shifted(grad_key.astype(jnp.bfloat16), "ctx", 1).astype(grad_key.dtype),
            shifted(grad_value.astype(jnp.bfloat16), "ctx", 1).astype(grad_value.dtype),
        )

    def cycle_step(cycle_turn, state_now):
        grad_query, key_block, value_block, grad_key, grad_value = state_now
        source = (cycle_index - cycle_turn) % cycle_size
        key_seg = lax.dynamic_slice_in_dim(all_seg, source * tok_rows, tok_rows)
        grad_query, key_part, value_part = grad_block(grad_query, key_block, value_block, key_seg)
        key_block, value_block = rotate_keys(key_block, value_block)
        grad_key, grad_value = rotate_grads(grad_key + key_part, grad_value + value_part)
        return (grad_query, key_block, value_block, grad_key, grad_value)

    zero_grads = jnp.zeros((tok_rows, model_width), jnp.float32)
    grad_query, key_block, value_block, grad_key, grad_value = lax.fori_loop(
        0, cycle_size - 1, cycle_step, (query_start, keys, values, zero_grads, zero_grads)
    )
    source = (cycle_index + 1) % cycle_size
    key_seg = lax.dynamic_slice_in_dim(all_seg, source * tok_rows, tok_rows)
    grad_query, key_part, value_part = grad_block(grad_query, key_block, value_block, key_seg)
    grad_key, grad_value = rotate_grads(grad_key + key_part, grad_value + value_part)
    query_flat = grad_query.reshape(tok_rows, model_width)
    d_query_bias = jnp.sum(query_flat, axis=0)
    d_value_bias = jnp.sum(grad_value, axis=0)
    d_qkv_low = jnp.concatenate([query_flat, grad_key, grad_value], axis=1).astype(jnp.bfloat16)
    d_qkv_weight = rows_product(normed, d_qkv_low)
    d_normed = cols_product(d_qkv_low, w_qkv)
    _, norm_one_back = jax.vjp(layer_norm, layer_in, gain_one, shift_one)
    d_in_norm, d_gain_one, d_shift_one = norm_one_back(d_normed)
    input_grad = (d_mid + d_in_norm).astype(jnp.bfloat16)
    attn_shards = (
        lax.psum_scatter(
            d_gain_one.astype(jnp.bfloat16), "fsdp", scatter_dimension=0, tiled=True
        ).astype(jnp.float32),
        lax.psum_scatter(
            d_shift_one.astype(jnp.bfloat16), "fsdp", scatter_dimension=0, tiled=True
        ).astype(jnp.float32),
        lax.psum_scatter(
            d_qkv_weight.astype(jnp.bfloat16), "fsdp", scatter_dimension=0, tiled=True
        ).astype(jnp.float32),
        lax.psum_scatter(
            d_query_bias.astype(jnp.bfloat16), "fsdp", scatter_dimension=0, tiled=True
        ).astype(jnp.float32),
        lax.psum_scatter(
            d_value_bias.astype(jnp.bfloat16), "fsdp", scatter_dimension=0, tiled=True
        ).astype(jnp.float32),
        lax.psum_scatter(
            d_out_weight.astype(jnp.bfloat16), "fsdp", scatter_dimension=0, tiled=True
        ).astype(jnp.float32),
        lax.psum_scatter(
            d_out_bias.astype(jnp.bfloat16), "fsdp", scatter_dimension=0, tiled=True
        ).astype(jnp.float32),
    )
    g_gain_one, g_shift_one, g_qkv, g_query, g_value, g_out_w, g_out_b = attn_shards
    g_gain_two, g_shift_two, g_up_w, g_up_b, g_down_w, g_down_b = mlp_shards
    summed = (
        lax.psum(g_gain_one.astype(jnp.bfloat16), "ctx").astype(jnp.float32),
        lax.psum(g_shift_one.astype(jnp.bfloat16), "ctx").astype(jnp.float32),
        lax.psum(g_qkv.astype(jnp.bfloat16), "ctx").astype(jnp.float32),
        lax.psum(g_query.astype(jnp.bfloat16), "ctx").astype(jnp.float32),
        lax.psum(g_value.astype(jnp.bfloat16), "ctx").astype(jnp.float32),
        lax.psum(g_out_w.astype(jnp.bfloat16), "ctx").astype(jnp.float32),
        lax.psum(g_out_b.astype(jnp.bfloat16), "ctx").astype(jnp.float32),
        lax.psum(g_gain_two.astype(jnp.bfloat16), "ctx").astype(jnp.float32),
        lax.psum(g_shift_two.astype(jnp.bfloat16), "ctx").astype(jnp.float32),
        lax.psum(g_up_w.astype(jnp.bfloat16), "ctx").astype(jnp.float32),
        lax.psum(g_up_b.astype(jnp.bfloat16), "ctx").astype(jnp.float32),
        lax.psum(g_down_w.astype(jnp.bfloat16), "ctx").astype(jnp.float32),
        lax.psum(g_down_b.astype(jnp.bfloat16), "ctx").astype(jnp.float32),
    )
    return (
        out_stream.astype(jnp.bfloat16)[None],
        input_grad[None],
        summed[0],
        summed[1],
        summed[2],
        summed[3],
        summed[4],
        summed[5],
        summed[6],
        summed[7],
        summed[8],
        summed[9],
        summed[10],
        summed[11],
        summed[12],
        stream_rms,
    )


def solution(mesh):
    return jax.shard_map(
        body,
        mesh=mesh,
        in_specs=(
            P("fsdp", "ctx", None),
            P("fsdp", "ctx"),
            P("fsdp", "ctx", None),
            P("fsdp"),
            P("fsdp"),
            P("fsdp", None),
            P("fsdp"),
            P("fsdp"),
            P("fsdp", None),
            P("fsdp"),
            P("fsdp"),
            P("fsdp"),
            P("fsdp", None),
            P("fsdp"),
            P("fsdp", None),
            P("fsdp"),
        ),
        out_specs=(
            P("fsdp", "ctx", None),
            P("fsdp", "ctx", None),
            P("fsdp"),
            P("fsdp"),
            P("fsdp", None),
            P("fsdp"),
            P("fsdp"),
            P("fsdp", None),
            P("fsdp"),
            P("fsdp"),
            P("fsdp"),
            P("fsdp", None),
            P("fsdp"),
            P("fsdp", None),
            P("fsdp"),
            P(),
        ),
        check_vma=False,
    )
```

profile of v0, /device:TPU:0, one launch (start us, length us, event | category | flops | bytes accessed | tf_op | source)
XLA Modules:
  0.0 1291.8 jit_solution(4417171927798934153)
XLA Ops:
  8.6 5.2 all-gather
  14.6 4.3 all-gather.1
  19.6 4.3 all-gather.2
  24.7 4.3 all-gather.3
  32.0 29.7 %all-gather.16.cloned.1.call-done = bf16[768,2304]{1,0:T(8,128)(2,1)} async-done(((bf16[384,2304]{1,0:T(8,128)(2,1)}), bf16[768,2304]{1,0:T(8,128)(2,1)}) %all-gather.16.cloned.1.call-update) | async-done | bytes 3538960 | tf_op jit(solution)/shard_map/all_gather | solution.py:69
  61.7 3.3 fusion.30
  68.7 22.1 %all_gather.48 = s32[1,4096]{1,0:T(1,128)} all-gather(s32[1,256]{1,0:T(1,128)} %param.21), channel_id=1, replica_groups=mesh['ctx'=16,'fsdp'=2] {'ctx'}, dimensions={1}, use_global_device_ids=true | all-gather | bytes 17408 | tf_op jit(solution)/shard_map/all_gather | solution.py:80
  93.3 4.3 all-gather.4
  98.3 4.3 all-gather.5
  103.2 4.3 all-gather.6
  108.2 4.5 all-gather.7
  118.6 9.5 all-gather.18.cloned.1.call-done
  128.1 63.3 %all-gather.20.cloned.1.call-done = bf16[4096,768]{1,0:T(8,128)(2,1)} async-done(((bf16[256,768]{1,0:T(8,128)(2,1)}), bf16[4096,768]{1,0:T(8,128)(2,1)}) %all-gather.20.cloned.1.call-update) | async-done | bytes 6291472 | tf_op jit(solution)/shard_map/all_gather | solution.py:123
  191.4 259.4 %while.39 = (s32[]{:T(128)}, f32[12,256]{1,0:T(8,128)}, f32[12,256]{1,0:T(8,128)}, f32[12,256,64]{1,2,0:T(8,128)}, s32[1,256]{1,0:T(1,128)}, /*index=5*/s32[16,2...) while((s32[]{:T(128)}, f32[12,256]{1,0:T(8,128)}, ...), condition=%wide.region_5.6_spmd.clone, body=%wide.region_2.5_spmd.clone.sunk | while | flops 210648064 | bytes 15798401 | solution.py:126
  454.4 5.5 convolution_add_fusion.1
  459.9 7.5 fusion.94
  480.3 445.9 %while.40 = (s32[]{:T(128)}, f32[256,12,64]{0,2,1:T(8,128)}, bf16[256,768]{0,1:T(8,128)(2,1)S(1)}, bf16[256,768]{0,1:T(8,128)(2,1)}, f32[256,768]{0,1:T(8,128)S(...) while((s32[]{:T(128)}, f32[256,12,64]{0,2,1:T(8,128)}, ...), condition=%wide.region_12.13_spmd.clone, body=%wide.region_11.12_spmd.clone.sunk | while | flops 513605632 | bytes 45556392 | solution.py:262
  498.5 3.2 collective-permute-done.3
  505.8 4.3 collective-permute-done.1
  522.3 4.9 collective-permute-done.2
  535.5 4.3 collective-permute-done.1
  551.0 5.9 collective-permute-done.2
  558.0 3.2 collective-permute-done.3
  565.2 4.3 collective-permute-done.1
  580.7 5.9 collective-permute-done.2
  587.7 3.2 collective-permute-done.3
  594.9 4.3 collective-permute-done.1
  610.4 5.9 collective-permute-done.2
  624.7 4.3 collective-permute-done.1
  640.1 5.9 collective-permute-done.2
  654.4 4.3 collective-permute-done.1
  669.9 5.9 collective-permute-done.2
  684.1 4.3 collective-permute-done.1
  699.6 5.9 collective-permute-done.2
  713.8 4.3 collective-permute-done.1
  729.3 5.9 collective-permute-done.2
  743.6 4.3 collective-permute-done.1
  759.0 5.9 collective-permute-done.2
  773.3 4.3 collective-permute-done.1
  788.7 5.9 collective-permute-done.2
  803.0 4.3 collective-permute-done.1
  818.5 5.9 collective-permute-done.2
  832.7 4.3 collective-permute-done.1
  848.2 5.9 collective-permute-done.2
  862.4 4.3 collective-permute-done.1
  877.9 5.9 collective-permute-done.2
  892.1 4.3 collective-permute-done.1
  907.6 5.9 collective-permute-done.2
  921.9 4.3 collective-permute-done.1
  933.6 6.4 collective-permute-done.4
  940.0 4.2 collective-permute-done.5
  949.0 4.4 convolution_convert_fusion.1
  954.5 6.3 convolution_convert_fusion
  960.9 31.3 %reduce-scatter.5.cloned.1.call-done = bf16[384,2304]{1,0:T(8,128)(2,1)} async-done(((bf16[768,2304]{1,0:T(8,128)(2,1)}), bf16[384,2304]{1,0:T(8,128)(2,1)}) %reduce-scatter.5.cloned.1.call-update) | async-done | bytes 1769488 | tf_op jit(solution)/shard_map/reduce_scatter | solution.py:285
  992.2 62.9 %reduce-scatter.9.cloned.1.call-done = bf16[384,3072]{1,0:T(8,128)(2,1)} async-done(((bf16[768,3072]{1,0:T(8,128)(2,1)}), bf16[384,3072]{1,0:T(8,128)(2,1)}) %reduce-scatter.9.cloned.1.call-update) | async-done | bytes 2359312 | tf_op jit(solution)/shard_map/reduce_scatter | solution.py:190
  1055.1 62.9 %reduce-scatter.11.cloned.1.call-done = bf16[1536,768]{1,0:T(8,128)(2,1)} async-done(((bf16[3072,768]{1,0:T(8,128)(2,1)}), bf16[1536,768]{1,0:T(8,128)(2,1)}) %reduce-scatter.11.cloned.1.call-update) | async-done | bytes 2359312 | tf_op jit(solution)/shard_map/reduce_scatter | solution.py:196
  1118.7 4.3 all-gather.8
  1127.5 3.5 fusion.69
  1131.0 6.0 fusion.89
  1139.1 41.8 %all-reduce.9 = (f32[3]{0:T(128)S(1)}, f32[]{:T(128)}) all-reduce(f32[3]{0:T(128)S(1)} %pad_maximum_fusion.4, f32[]{:T(128)} %fusion.78), channel_id=1, replica_groups=mesh['ctx'=16,'fsdp'=2] {'ctx','fsdp'}, use_global_device_ids=true, to_apply=%region_53.54 | all-reduce | flops 4 | bytes 32 | tf_op jit(solution)/shard_map/psum | solution.py:168
  1184.9 9.1 all-reduce.12
  1194.6 58.7 %all-reduce.10 = (bf16[384]{0:T(512)(128)(2,1)S(1)}, bf16[384]{0:T(512)(128)(2,1)S(1)}, bf16[384]{0:T(512)(128)(2,1)S(1)}, bf16[384]{0:T(512)(128)(2,1)S(1)}, bf...) all-reduce(bf16[384]{0:T(512)(128)(2,1)S(1)} %dynamic-slice.2, ...), channel_id=1, replica_groups=mesh['ctx'=16,'fsdp'=2] {'ctx'}, use_global_device_ids=true, to_apply=%region_17.18 | all-reduce | flops 4608 | bytes 18432 | tf_op jit(solution)/shard_map/psum | solution.py:304
  1259.7 15.3 %all-reduce.15.cloned.1.call-done = (bf16[384,2304]{1,0:T(8,128)(2,1)}, bf16[384,768]{1,0:T(8,128)(2,1)}, bf16[384,3072]{1,0:T(8,128)(2,1)}, bf16[1536,768]{1,0:T(8,128)(2,1)}) async-done(((bf16[384,2304]{1,0:T(8,128)(2,1)}, bf16[384,768]{1,0:T(8,128)(2,1)}, bf16[384,3072]{1,0:T(8,128)(2,1)}, bf16[1536,768]{1,0:T(8,128)(2,1)}), (bf16[384,2304]{1,0:T(8,128)(2,1)}, bf16[384,768]{1,0:T(8,128)(2,1)}, ...) | async-done | bytes 7077904 | tf_op jit(solution)/shard_map/psum | solution.py:306
  1275.0 4.6 convert_element_type.311
  (897 shorter events, 618.8 us)
Async XLA Ops:
  7.2 54.5 %all-gather.16.cloned.1.call-start = ((), (), s32[]{:S(2)}) async-start(), calls=%async_computation.4 | async-start | bytes 5308416 | tf_op jit(solution)/shard_map/all_gather | solution.py:69
  7.9 120.2 %all-gather.18.cloned.1.call-start = ((), (), s32[]{:S(2)}) async-start(), calls=%async_computation.5 | async-start | bytes 6684672 | tf_op jit(solution)/shard_map/all_gather | solution.py:122
  66.1 125.4 %all-gather.20.cloned.1.call-start = ((), (), s32[]{:S(2)}) async-start(), calls=%async_computation.6 | async-start | bytes 6684672 | tf_op jit(solution)/shard_map/all_gather | solution.py:123
  66.8 385.3 %all-gather.22.cloned.1.call-start = ((), (), s32[]{:S(2)}) async-start(), calls=%async_computation.7 | async-start | bytes 1769472 | tf_op jit(solution)/shard_map/all_gather | solution.py:72
  67.4 387.0 %all-gather.24.cloned.1.call-start = ((), (), s32[]{:S(2)}) async-start(), calls=%async_computation.8 | async-start | bytes 7077888 | tf_op jit(solution)/shard_map/all_gather | solution.py:142
  68.0 392.0 %all-gather.26.cloned.1.call-start = ((), (), s32[]{:S(2)}) async-start(), calls=%async_computation.9 | async-start | bytes 7077888 | tf_op jit(solution)/shard_map/all_gather | solution.py:144
  68.5 892.3 %reduce-scatter.7.cloned.1.call-start = ((), (), s32[]{:S(2)}) async-start(), calls=%async_computation.11 | async-start | bytes 1769472 | tf_op jit(solution)/shard_map/reduce_scatter | solution.py:294
  480.0 512.2 %reduce-scatter.5.cloned.1.call-start = ((), (), s32[]{:S(2)}) async-start(), calls=%async_computation.10 | async-start | bytes 5308416 | tf_op jit(solution)/shard_map/reduce_scatter | solution.py:285
  487.2 10.2 collective-permute-start.2
  490.1 11.5 collective-permute-start.3
  490.4 15.3 %collective-permute-start = (bf16[256,768]{0,1:T(8,128)(2,1)S(1)}, bf16[256,768]{0,1:T(8,128)(2,1)S(1)}, u32[]{:S(2)}, u32[]{:S(2)}) collective-permute-start(bf16[256,768]{0,1:T(8,128)(2,1)S(1)} %copy.86), channel_id=1, source_target_pairs={{30,0},{0,2},{2,4},{4,6},{6,8},{8,10},{10,12},{12,14},{14,16},{16,... | collective-permute-start | bytes 1179656 | tf_op jit(solution)/shard_map/while/body/eval_jaxpr/ppermute | solution.py:17
  490.7 19.4 %collective-permute-start.1 = (bf16[256,768]{0,1:T(8,128)(2,1)}, bf16[256,768]{0,1:T(8,128)(2,1)}, u32[]{:S(2)}, u32[]{:S(2)}) collective-permute-start(bf16[256,768]{0,1:T(8,128)(2,1)} %copy-done.11), channel_id=1, source_target_pairs={{30,0},{0,2},{2,4},{4,6},{6,8},{8,10},{10,12},{12,14},{14,16},{16,... | collective-permute-start | bytes 1179656 | tf_op jit(solution)/shard_map/while/body/eval_jaxpr/ppermute | solution.py:17
  519.7 11.7 collective-permute-start.3
  519.7 15.8 %collective-permute-start = (bf16[256,768]{0,1:T(8,128)(2,1)S(1)}, bf16[256,768]{0,1:T(8,128)(2,1)S(1)}, u32[]{:S(2)}, u32[]{:S(2)}) collective-permute-start(bf16[256,768]{0,1:T(8,128)(2,1)S(1)} %copy.86), channel_id=1, source_target_pairs={{30,0},{0,2},{2,4},{4,6},{6,8},{8,10},{10,12},{12,14},{14,16},{16,... | collective-permute-start | bytes 1179656 | tf_op jit(solution)/shard_map/while/body/eval_jaxpr/ppermute | solution.py:17
  519.7 20.1 %collective-permute-start.1 = (bf16[256,768]{0,1:T(8,128)(2,1)}, bf16[256,768]{0,1:T(8,128)(2,1)}, u32[]{:S(2)}, u32[]{:S(2)}) collective-permute-start(bf16[256,768]{0,1:T(8,128)(2,1)} %copy-done.11), channel_id=1, source_target_pairs={{30,0},{0,2},{2,4},{4,6},{6,8},{8,10},{10,12},{12,14},{14,16},{16,... | collective-permute-start | bytes 1179656 | tf_op jit(solution)/shard_map/while/body/eval_jaxpr/ppermute | solution.py:17
  546.7 10.2 collective-permute-start.2
  549.4 11.7 collective-permute-start.3
  549.4 15.8 %collective-permute-start = (bf16[256,768]{0,1:T(8,128)(2,1)S(1)}, bf16[256,768]{0,1:T(8,128)(2,1)S(1)}, u32[]{:S(2)}, u32[]{:S(2)}) collective-permute-start(bf16[256,768]{0,1:T(8,128)(2,1)S(1)} %copy.86), channel_id=1, source_target_pairs={{30,0},{0,2},{2,4},{4,6},{6,8},{8,10},{10,12},{12,14},{14,16},{16,... | collective-permute-start | bytes 1179656 | tf_op jit(solution)/shard_map/while/body/eval_jaxpr/ppermute | solution.py:17
  549.4 20.1 %collective-permute-start.1 = (bf16[256,768]{0,1:T(8,128)(2,1)}, bf16[256,768]{0,1:T(8,128)(2,1)}, u32[]{:S(2)}, u32[]{:S(2)}) collective-permute-start(bf16[256,768]{0,1:T(8,128)(2,1)} %copy-done.11), channel_id=1, source_target_pairs={{30,0},{0,2},{2,4},{4,6},{6,8},{8,10},{10,12},{12,14},{14,16},{16,... | collective-permute-start | bytes 1179656 | tf_op jit(solution)/shard_map/while/body/eval_jaxpr/ppermute | solution.py:17
  576.4 10.2 collective-permute-start.2
  579.1 11.7 collective-permute-start.3
  579.1 15.8 %collective-permute-start = (bf16[256,768]{0,1:T(8,128)(2,1)S(1)}, bf16[256,768]{0,1:T(8,128)(2,1)S(1)}, u32[]{:S(2)}, u32[]{:S(2)}) collective-permute-start(bf16[256,768]{0,1:T(8,128)(2,1)S(1)} %copy.86), channel_id=1, source_target_pairs={{30,0},{0,2},{2,4},{4,6},{6,8},{8,10},{10,12},{12,14},{14,16},{16,... | collective-permute-start | bytes 1179656 | tf_op jit(solution)/shard_map/while/body/eval_jaxpr/ppermute | solution.py:17
  579.1 20.1 %collective-permute-start.1 = (bf16[256,768]{0,1:T(8,128)(2,1)}, bf16[256,768]{0,1:T(8,128)(2,1)}, u32[]{:S(2)}, u32[]{:S(2)}) collective-permute-start(bf16[256,768]{0,1:T(8,128)(2,1)} %copy-done.11), channel_id=1, source_target_pairs={{30,0},{0,2},{2,4},{4,6},{6,8},{8,10},{10,12},{12,14},{14,16},{16,... | collective-permute-start | bytes 1179656 | tf_op jit(solution)/shard_map/while/body/eval_jaxpr/ppermute | solution.py:17
  608.9 11.7 collective-permute-start.3
  608.9 15.8 %collective-permute-start = (bf16[256,768]{0,1:T(8,128)(2,1)S(1)}, bf16[256,768]{0,1:T(8,128)(2,1)S(1)}, u32[]{:S(2)}, u32[]{:S(2)}) collective-permute-start(bf16[256,768]{0,1:T(8,128)(2,1)S(1)} %copy.86), channel_id=1, source_target_pairs={{30,0},{0,2},{2,4},{4,6},{6,8},{8,10},{10,12},{12,14},{14,16},{16,... | collective-permute-start | bytes 1179656 | tf_op jit(solution)/shard_map/while/body/eval_jaxpr/ppermute | solution.py:17
  608.9 20.1 %collective-permute-start.1 = (bf16[256,768]{0,1:T(8,128)(2,1)}, bf16[256,768]{0,1:T(8,128)(2,1)}, u32[]{:S(2)}, u32[]{:S(2)}) collective-permute-start(bf16[256,768]{0,1:T(8,128)(2,1)} %copy-done.11), channel_id=1, source_target_pairs={{30,0},{0,2},{2,4},{4,6},{6,8},{8,10},{10,12},{12,14},{14,16},{16,... | collective-permute-start | bytes 1179656 | tf_op jit(solution)/shard_map/while/body/eval_jaxpr/ppermute | solution.py:17
  635.8 10.2 collective-permute-start.2
  638.6 11.7 collective-permute-start.3
  638.6 15.8 %collective-permute-start = (bf16[256,768]{0,1:T(8,128)(2,1)S(1)}, bf16[256,768]{0,1:T(8,128)(2,1)S(1)}, u32[]{:S(2)}, u32[]{:S(2)}) collective-permute-start(bf16[256,768]{0,1:T(8,128)(2,1)S(1)} %copy.86), channel_id=1, source_target_pairs={{30,0},{0,2},{2,4},{4,6},{6,8},{8,10},{10,12},{12,14},{14,16},{16,... | collective-permute-start | bytes 1179656 | tf_op jit(solution)/shard_map/while/body/eval_jaxpr/ppermute | solution.py:17
  638.6 20.1 %collective-permute-start.1 = (bf16[256,768]{0,1:T(8,128)(2,1)}, bf16[256,768]{0,1:T(8,128)(2,1)}, u32[]{:S(2)}, u32[]{:S(2)}) collective-permute-start(bf16[256,768]{0,1:T(8,128)(2,1)} %copy-done.11), channel_id=1, source_target_pairs={{30,0},{0,2},{2,4},{4,6},{6,8},{8,10},{10,12},{12,14},{14,16},{16,... | collective-permute-start | bytes 1179656 | tf_op jit(solution)/shard_map/while/body/eval_jaxpr/ppermute | solution.py:17
  665.6 10.2 collective-permute-start.2
  668.3 11.7 collective-permute-start.3
  668.3 15.8 %collective-permute-start = (bf16[256,768]{0,1:T(8,128)(2,1)S(1)}, bf16[256,768]{0,1:T(8,128)(2,1)S(1)}, u32[]{:S(2)}, u32[]{:S(2)}) collective-permute-start(bf16[256,768]{0,1:T(8,128)(2,1)S(1)} %copy.86), channel_id=1, source_target_pairs={{30,0},{0,2},{2,4},{4,6},{6,8},{8,10},{10,12},{12,14},{14,16},{16,... | collective-permute-start | bytes 1179656 | tf_op jit(solution)/shard_map/while/body/eval_jaxpr/ppermute | solution.py:17
  668.3 20.1 %collective-permute-start.1 = (bf16[256,768]{0,1:T(8,128)(2,1)}, bf16[256,768]{0,1:T(8,128)(2,1)}, u32[]{:S(2)}, u32[]{:S(2)}) collective-permute-start(bf16[256,768]{0,1:T(8,128)(2,1)} %copy-done.11), channel_id=1, source_target_pairs={{30,0},{0,2},{2,4},{4,6},{6,8},{8,10},{10,12},{12,14},{14,16},{16,... | collective-permute-start | bytes 1179656 | tf_op jit(solution)/shard_map/while/body/eval_jaxpr/ppermute | solution.py:17
  695.3 10.2 collective-permute-start.2
  698.0 11.7 collective-permute-start.3
  698.0 15.8 %collective-permute-start = (bf16[256,768]{0,1:T(8,128)(2,1)S(1)}, bf16[256,768]{0,1:T(8,128)(2,1)S(1)}, u32[]{:S(2)}, u32[]{:S(2)}) collective-permute-start(bf16[256,768]{0,1:T(8,128)(2,1)S(1)} %copy.86), channel_id=1, source_target_pairs={{30,0},{0,2},{2,4},{4,6},{6,8},{8,10},{10,12},{12,14},{14,16},{16,... | collective-permute-start | bytes 1179656 | tf_op jit(solution)/shard_map/while/body/eval_jaxpr/ppermute | solution.py:17
  698.0 20.1 %collective-permute-start.1 = (bf16[256,768]{0,1:T(8,128)(2,1)}, bf16[256,768]{0,1:T(8,128)(2,1)}, u32[]{:S(2)}, u32[]{:S(2)}) collective-permute-start(bf16[256,768]{0,1:T(8,128)(2,1)} %copy-done.11), channel_id=1, source_target_pairs={{30,0},{0,2},{2,4},{4,6},{6,8},{8,10},{10,12},{12,14},{14,16},{16,... | collective-permute-start | bytes 1179656 | tf_op jit(solution)/shard_map/while/body/eval_jaxpr/ppermute | solution.py:17
  725.0 10.2 collective-permute-start.2
  727.8 11.7 collective-permute-start.3
  727.8 15.8 %collective-permute-start = (bf16[256,768]{0,1:T(8,128)(2,1)S(1)}, bf16[256,768]{0,1:T(8,128)(2,1)S(1)}, u32[]{:S(2)}, u32[]{:S(2)}) collective-permute-start(bf16[256,768]{0,1:T(8,128)(2,1)S(1)} %copy.86), channel_id=1, source_target_pairs={{30,0},{0,2},{2,4},{4,6},{6,8},{8,10},{10,12},{12,14},{14,16},{16,... | collective-permute-start | bytes 1179656 | tf_op jit(solution)/shard_map/while/body/eval_jaxpr/ppermute | solution.py:17
  727.8 20.1 %collective-permute-start.1 = (bf16[256,768]{0,1:T(8,128)(2,1)}, bf16[256,768]{0,1:T(8,128)(2,1)}, u32[]{:S(2)}, u32[]{:S(2)}) collective-permute-start(bf16[256,768]{0,1:T(8,128)(2,1)} %copy-done.11), channel_id=1, source_target_pairs={{30,0},{0,2},{2,4},{4,6},{6,8},{8,10},{10,12},{12,14},{14,16},{16,... | collective-permute-start | bytes 1179656 | tf_op jit(solution)/shard_map/while/body/eval_jaxpr/ppermute | solution.py:17
  757.5 11.7 collective-permute-start.3
  757.5 15.8 %collective-permute-start = (bf16[256,768]{0,1:T(8,128)(2,1)S(1)}, bf16[256,768]{0,1:T(8,128)(2,1)S(1)}, u32[]{:S(2)}, u32[]{:S(2)}) collective-permute-start(bf16[256,768]{0,1:T(8,128)(2,1)S(1)} %copy.86), channel_id=1, source_target_pairs={{30,0},{0,2},{2,4},{4,6},{6,8},{8,10},{10,12},{12,14},{14,16},{16,... | collective-permute-start | bytes 1179656 | tf_op jit(solution)/shard_map/while/body/eval_jaxpr/ppermute | solution.py:17
  757.5 20.1 %collective-permute-start.1 = (bf16[256,768]{0,1:T(8,128)(2,1)}, bf16[256,768]{0,1:T(8,128)(2,1)}, u32[]{:S(2)}, u32[]{:S(2)}) collective-permute-start(bf16[256,768]{0,1:T(8,128)(2,1)} %copy-done.11), channel_id=1, source_target_pairs={{30,0},{0,2},{2,4},{4,6},{6,8},{8,10},{10,12},{12,14},{14,16},{16,... | collective-permute-start | bytes 1179656 | tf_op jit(solution)/shard_map/while/body/eval_jaxpr/ppermute | solution.py:17
  787.2 11.7 collective-permute-start.3
  787.2 15.8 %collective-permute-start = (bf16[256,768]{0,1:T(8,128)(2,1)S(1)}, bf16[256,768]{0,1:T(8,128)(2,1)S(1)}, u32[]{:S(2)}, u32[]{:S(2)}) collective-permute-start(bf16[256,768]{0,1:T(8,128)(2,1)S(1)} %copy.86), channel_id=1, source_target_pairs={{30,0},{0,2},{2,4},{4,6},{6,8},{8,10},{10,12},{12,14},{14,16},{16,... | collective-permute-start | bytes 1179656 | tf_op jit(solution)/shard_map/while/body/eval_jaxpr/ppermute | solution.py:17
  787.2 20.1 %collective-permute-start.1 = (bf16[256,768]{0,1:T(8,128)(2,1)}, bf16[256,768]{0,1:T(8,128)(2,1)}, u32[]{:S(2)}, u32[]{:S(2)}) collective-permute-start(bf16[256,768]{0,1:T(8,128)(2,1)} %copy-done.11), channel_id=1, source_target_pairs={{30,0},{0,2},{2,4},{4,6},{6,8},{8,10},{10,12},{12,14},{14,16},{16,... | collective-permute-start | bytes 1179656 | tf_op jit(solution)/shard_map/while/body/eval_jaxpr/ppermute | solution.py:17
  816.9 11.7 collective-permute-start.3
  816.9 15.8 %collective-permute-start = (bf16[256,768]{0,1:T(8,128)(2,1)S(1)}, bf16[256,768]{0,1:T(8,128)(2,1)S(1)}, u32[]{:S(2)}, u32[]{:S(2)}) collective-permute-start(bf16[256,768]{0,1:T(8,128)(2,1)S(1)} %copy.86), channel_id=1, source_target_pairs={{30,0},{0,2},{2,4},{4,6},{6,8},{8,10},{10,12},{12,14},{14,16},{16,... | collective-permute-start | bytes 1179656 | tf_op jit(solution)/shard_map/while/body/eval_jaxpr/ppermute | solution.py:17
  816.9 20.1 %collective-permute-start.1 = (bf16[256,768]{0,1:T(8,128)(2,1)}, bf16[256,768]{0,1:T(8,128)(2,1)}, u32[]{:S(2)}, u32[]{:S(2)}) collective-permute-start(bf16[256,768]{0,1:T(8,128)(2,1)} %copy-done.11), channel_id=1, source_target_pairs={{30,0},{0,2},{2,4},{4,6},{6,8},{8,10},{10,12},{12,14},{14,16},{16,... | collective-permute-start | bytes 1179656 | tf_op jit(solution)/shard_map/while/body/eval_jaxpr/ppermute | solution.py:17
  846.6 11.7 collective-permute-start.3
  846.6 15.8 %collective-permute-start = (bf16[256,768]{0,1:T(8,128)(2,1)S(1)}, bf16[256,768]{0,1:T(8,128)(2,1)S(1)}, u32[]{:S(2)}, u32[]{:S(2)}) collective-permute-start(bf16[256,768]{0,1:T(8,128)(2,1)S(1)} %copy.86), channel_id=1, source_target_pairs={{30,0},{0,2},{2,4},{4,6},{6,8},{8,10},{10,12},{12,14},{14,16},{16,... | collective-permute-start | bytes 1179656 | tf_op jit(solution)/shard_map/while/body/eval_jaxpr/ppermute | solution.py:17
  846.6 20.1 %collective-permute-start.1 = (bf16[256,768]{0,1:T(8,128)(2,1)}, bf16[256,768]{0,1:T(8,128)(2,1)}, u32[]{:S(2)}, u32[]{:S(2)}) collective-permute-start(bf16[256,768]{0,1:T(8,128)(2,1)} %copy-done.11), channel_id=1, source_target_pairs={{30,0},{0,2},{2,4},{4,6},{6,8},{8,10},{10,12},{12,14},{14,16},{16,... | collective-permute-start | bytes 1179656 | tf_op jit(solution)/shard_map/while/body/eval_jaxpr/ppermute | solution.py:17
  876.4 11.7 collective-permute-start.3
  876.4 15.8 %collective-permute-start = (bf16[256,768]{0,1:T(8,128)(2,1)S(1)}, bf16[256,768]{0,1:T(8,128)(2,1)S(1)}, u32[]{:S(2)}, u32[]{:S(2)}) collective-permute-start(bf16[256,768]{0,1:T(8,128)(2,1)S(1)} %copy.86), channel_id=1, source_target_pairs={{30,0},{0,2},{2,4},{4,6},{6,8},{8,10},{10,12},{12,14},{14,16},{16,... | collective-permute-start | bytes 1179656 | tf_op jit(solution)/shard_map/while/body/eval_jaxpr/ppermute | solution.py:17
  876.4 20.1 %collective-permute-start.1 = (bf16[256,768]{0,1:T(8,128)(2,1)}, bf16[256,768]{0,1:T(8,128)(2,1)}, u32[]{:S(2)}, u32[]{:S(2)}) collective-permute-start(bf16[256,768]{0,1:T(8,128)(2,1)} %copy-done.11), channel_id=1, source_target_pairs={{30,0},{0,2},{2,4},{4,6},{6,8},{8,10},{10,12},{12,14},{14,16},{16,... | collective-permute-start | bytes 1179656 | tf_op jit(solution)/shard_map/while/body/eval_jaxpr/ppermute | solution.py:17
  906.1 11.7 collective-permute-start.3
  906.1 15.8 %collective-permute-start = (bf16[256,768]{0,1:T(8,128)(2,1)S(1)}, bf16[256,768]{0,1:T(8,128)(2,1)S(1)}, u32[]{:S(2)}, u32[]{:S(2)}) collective-permute-start(bf16[256,768]{0,1:T(8,128)(2,1)S(1)} %copy.86), channel_id=1, source_target_pairs={{30,0},{0,2},{2,4},{4,6},{6,8},{8,10},{10,12},{12,14},{14,16},{16,... | collective-permute-start | bytes 1179656 | tf_op jit(solution)/shard_map/while/body/eval_jaxpr/ppermute | solution.py:17
  906.1 20.1 %collective-permute-start.1 = (bf16[256,768]{0,1:T(8,128)(2,1)}, bf16[256,768]{0,1:T(8,128)(2,1)}, u32[]{:S(2)}, u32[]{:S(2)}) collective-permute-start(bf16[256,768]{0,1:T(8,128)(2,1)} %copy-done.11), channel_id=1, source_target_pairs={{30,0},{0,2},{2,4},{4,6},{6,8},{8,10},{10,12},{12,14},{14,16},{16,... | collective-permute-start | bytes 1179656 | tf_op jit(solution)/shard_map/while/body/eval_jaxpr/ppermute | solution.py:17
  932.2 12.0 collective-permute-start.5
  947.4 107.7 %reduce-scatter.9.cloned.1.call-start = ((), (), s32[]{:S(2)}) async-start(), calls=%async_computation.12 | async-start | bytes 7077888 | tf_op jit(solution)/shard_map/reduce_scatter | solution.py:190
  953.5 164.5 %reduce-scatter.11.cloned.1.call-start = ((), (), s32[]{:S(2)}) async-start(), calls=%async_computation.13 | async-start | bytes 7077888 | tf_op jit(solution)/shard_map/reduce_scatter | solution.py:196
  960.8 314.2 %all-reduce.15.cloned.1.call-start = ((), (), s32[]{:S(2)}) async-start(), calls=%async_computation.14 | async-start | bytes 14155776 | tf_op jit(solution)/shard_map/psum | solution.py:306
  (163 other events, 1614.7 us)
Sparse Core Ops, SparseCore 0:
  9.6 52.0 all-gather.15
  66.2 61.8 all-gather.17
  131.0 60.4 all-gather.19
  192.8 21.3 all-gather.21
  215.6 62.6 all-gather.23
  279.7 62.6 all-gather.25
  480.1 20.2 reduce-scatter.6
  947.5 44.6 reduce-scatter.4
  995.1 59.9 reduce-scatter.8
  1057.9 59.9 reduce-scatter.10
  1122.0 152.9 all-reduce.14
where the time goes:
time: 1300 us; the launch traced here: 1290 us
  waiting for transfers between devices  518 us (40%)
  matrix products  225 us (17%)
  other arithmetic  199 us (15%)
  blocking collectives  172 us (13%)
  local copies, waits for them, and re-layouts  155 us (12%)
  between operations  16.6 us (1%)
    ppermute x62, waiting for transfers between devices, shifted(): return lax.ppermute(block, axis, route)  240 us
    dynamic_slice x64, local copies, waits for them, and re-layouts, body(): lax.scan(attend_step, state_now, (key_piece.reshape(blocks, tok_rows, mod...  87.2 us
    all_gather x1, waiting for transfers between devices, body(): value_piece = lax.all_gather(values, 'ctx', axis=0, tiled=True)  63.3 us
    reduce_scatter x1, waiting for transfers between devices, body(): lax.psum_scatter(d_up_weight.astype(jnp.bfloat16), 'fsdp', scatter_dimens...  62.9 us
    reduce_scatter x1, waiting for transfers between devices, body(): lax.psum_scatter(d_down_weight.astype(jnp.bfloat16), 'fsdp', scatter_dime...  62.9 us
    psum x1, blocking collectives, body(): lax.psum(g_gain_one.astype(jnp.bfloat16), 'ctx').astype(jnp.float32)  58.7 us
    dot_general x16, matrix products, attend(): jnp.einsum('hqk,khd->hqd', weights.astype(jnp.bfloat16), value_heads, pre...  46.2 us
    psum x1, blocking collectives, body(): square_sums, count_sum = lax.psum((squares, counted), ('ctx', 'fsdp'))  41.8 us
  transfers between devices with their start and end apart: 73, of which 69 were waited for; matrix products, arithmetic and copies ran while one was open for 41% of the time, Pallas kernels for 0%

commit v1 on v0

v1 whole, which is shorter than its diff:
```python
import math

import jax
import jax.numpy as jnp
from jax import lax
from jax.experimental import pallas as pl
from jax.experimental.pallas import tpu as pltpu
from jax.sharding import PartitionSpec as P

D = 768
HEADS = 12
HEAD_DIM = 64
FF = 3072
EPS = 1e-06
GROUPS = 4
GH = HEADS // GROUPS
GW = GH * HEAD_DIM
FAR = -(2.0**100)
LOG2E = math.log2(math.e)
BF = jnp.bfloat16
F32 = jnp.float32


def swap(block, axis, mask):
    size = lax.axis_size(axis)
    return lax.ppermute(block, axis, [(i, i ^ mask) for i in range(size)])


def gather(blocks, axis, masks):
    for mask in masks:
        blocks = jnp.concatenate([blocks, swap(blocks, axis, mask)], axis=0)
    return blocks


def reduce_blocks(blocks, axis, masks):
    for mask in reversed(masks):
        half = blocks.shape[0] // 2
        got = swap(blocks[half:], axis, mask)
        blocks = (blocks[:half].astype(F32) + got.astype(F32)).astype(BF)
    return blocks


def orders(masks):
    out = [0]
    for mask in masks:
        out = out + [d ^ mask for d in out]
    return out


def arranged(blocks, distances, me, unit=1):
    n = len(distances)
    if n == 2:
        return jnp.where(me == 0, blocks, blocks[::-1])
    place = [distances.index(d * unit) for d in range(n)]
    table = jnp.array(place, jnp.int32)
    return jnp.stack(
        [lax.dynamic_index_in_dim(blocks, table[a ^ me], 0, keepdims=False) for a in range(n)]
    )


def rows_product(left, right):
    return lax.dot_general(
        left, right, (((0,), (0,)), ((), ())), preferred_element_type=F32
    )


def cols_product(left, right):
    return lax.dot_general(
        left, right, (((1,), (1,)), ((), ())), preferred_element_type=F32
    )


def standard(inputs):
    row_mean = jnp.mean(inputs, axis=-1, keepdims=True)
    centred = inputs - row_mean
    variance = jnp.mean(centred * centred, axis=-1, keepdims=True)
    scale = lax.rsqrt(variance + EPS)
    return centred * scale, scale


def standard_back(grad, unit, scale):
    return scale * (
        grad
        - jnp.mean(grad, axis=-1, keepdims=True)
        - unit * jnp.mean(grad * unit, axis=-1, keepdims=True)
    )


def gelu_tanh(inputs):
    return jax.nn.gelu(inputs, approximate=True)


def three_parts(value):
    top = value.astype(BF).astype(F32)
    rest = value - top
    middle = rest.astype(BF).astype(F32)
    return top, middle, rest - middle


def query_side(head_t, extra):
    return jnp.concatenate([head_t, extra.astype(BF)], axis=0)


def forward_kernel(tiles, q_ref, k_ref, v_ref, mark_ref, seg_ref, ft_ref, low_ref, log_ref, q_s, m_s, acc_s):
    step = pl.program_id(0)
    n_q = q_ref.shape[0]

    @pl.when(step == 0)
    def _():
        q_t = q_ref[...].T
        row = lax.broadcasted_iota(jnp.int32, (HEAD_DIM, n_q), 0)
        away = (row < 8) & (row.astype(F32) != seg_ref[...])
        extra = jnp.where(away, FAR, 0.0)
        for h in range(GH):
            q_s[h] = query_side(q_t[h * HEAD_DIM : (h + 1) * HEAD_DIM], extra)
        m_s[...] = jnp.full_like(m_s, 2 * FAR)
        acc_s[...] = jnp.zeros_like(acc_s)

    v_t = v_ref[...].T
    ones = jnp.ones((16, v_t.shape[1]), BF)
    for h in range(GH):
        mine = slice(h * HEAD_DIM, (h + 1) * HEAD_DIM)
        keys = jnp.concatenate([k_ref[:, mine], mark_ref[...]], axis=1)
        scores = jnp.dot(keys, q_s[h], preferred_element_type=F32)
        old = m_s[h]
        new = jnp.maximum(old, jnp.max(scores, axis=0, keepdims=True))
        weights = jnp.exp2(scores - new)
        m_s[h] = new
        values = jnp.concatenate([v_t[mine], ones], axis=0)
        acc_s[h] = acc_s[h] * jnp.exp2(old - new) + jnp.dot(
            values, weights.astype(BF), preferred_element_type=F32
        )

    @pl.when(step == pl.num_programs(0) - 1)
    def _():
        parts = []
        for h in range(GH):
            total = acc_s[h, HEAD_DIM : HEAD_DIM + 1]
            parts.append(acc_s[h, :HEAD_DIM] / total)
            log_ref[h] = m_s[h] + jnp.log2(total)
        whole = jnp.concatenate(parts, axis=0)
        ft_ref[...] = whole
        low_ref[...] = whole.astype(BF).T


def forward_attention(q, k, v, mark, seg_row):
    n_q, n_k = q.shape[0], k.shape[0]
    block = 1024
    return pl.pallas_call(
        lambda *refs: forward_kernel(n_k // block, *refs),
        name="attention_forward",
        grid=(n_k // block,),
        in_specs=[
            pl.BlockSpec((n_q, GW), lambda i: (0, 0)),
            pl.BlockSpec((block, GW), lambda i: (i, 0)),
            pl.BlockSpec((block, GW), lambda i: (i, 0)),
            pl.BlockSpec((block, HEAD_DIM), lambda i: (i, 0)),
            pl.BlockSpec((1, n_q), lambda i: (0, 0)),
        ],
        out_specs=[
            pl.BlockSpec((GW, n_q), lambda i: (0, 0)),
            pl.BlockSpec((n_q, GW), lambda i: (0, 0)),
            pl.BlockSpec((GH, 1, n_q), lambda i: (0, 0, 0)),
        ],
        out_shape=[
            jax.ShapeDtypeStruct((GW, n_q), F32),
            jax.ShapeDtypeStruct((n_q, GW), BF),
            jax.ShapeDtypeStruct((GH, 1, n_q), F32),
        ],
        scratch_shapes=[
            pltpu.VMEM((GH, 2 * HEAD_DIM, n_q), BF),
            pltpu.VMEM((GH, 1, n_q), F32),
            pltpu.VMEM((GH, HEAD_DIM + 16, n_q), F32),
        ],
        compiler_params=pltpu.CompilerParams(vmem_limit_bytes=30 * 1024 * 1024),
        cost_estimate=pl.CostEstimate(
            flops=4 * n_q * n_k * 256 * GH, bytes_accessed=8 << 20, transcendentals=GH * n_q * n_k
        ),
    )(q, k, v, mark, seg_row)


def backward_kernel(
    q_ref, g_ref, ft_ref, log_ref, seg_ref, k_ref, v_ref, mark_ref,
    dq_ref, dk_ref, dv_ref, sum_ref, q_s, g_s, dq_s,
):
    step = pl.program_id(0)
    n_q = q_ref.shape[0]

    @pl.when(step == 0)
    def _():
        q_t = q_ref[...].T
        g_t = g_ref[...].T
        row = lax.broadcasted_iota(jnp.int32, (HEAD_DIM, n_q), 0)
        away = jnp.where((row < 8) & (row.astype(F32) != seg_ref[...]), FAR, 0.0)

        def with_parts(base, value):
            top, middle, low = three_parts(value)
            base = jnp.where(row == 8, -top, base)
            base = jnp.where(row == 9, -middle, base)
            return jnp.where(row == 10, -low, base)

        for h in range(GH):
            mine = slice(h * HEAD_DIM, (h + 1) * HEAD_DIM)
            q_s[h] = query_side(q_t[mine], with_parts(away, log_ref[h]))
            delta = jnp.sum(g_t[mine].astype(F32) * ft_ref[mine], axis=0, keepdims=True)
            g_s[h] = query_side(g_t[mine], with_parts(jnp.zeros_like(away), delta))
        dq_s[...] = jnp.zeros_like(dq_s)

    k_t = k_ref[...].T
    dks, dvs = [], []
    for h in range(GH):
        mine = slice(h * HEAD_DIM, (h + 1) * HEAD_DIM)
        keys = jnp.concatenate([k_ref[:, mine], mark_ref[...]], axis=1)
        values = jnp.concatenate([v_ref[:, mine], mark_ref[...]], axis=1)
        probs = jnp.exp2(jnp.dot(keys, q_s[h], preferred_element_type=F32))
        d_probs = jnp.dot(values, g_s[h], preferred_element_type=F32)
        d_scores = (probs * d_probs).astype(BF)
        dvs.append(jnp.dot(probs.astype(BF), g_ref[:, mine], preferred_element_type=F32))
        dks.append(jnp.dot(d_scores, q_ref[:, mine], preferred_element_type=F32))
        dq_s[mine] += jnp.dot(k_t[mine], d_scores, preferred_element_type=F32)
    dk_ref[...] = (jnp.concatenate(dks, axis=1) * (1.0 / LOG2E)).astype(BF)
    dv_ref[...] = jnp.concatenate(dvs, axis=1).astype(BF)

    @pl.when(step == pl.num_programs(0) - 1)
    def _():
        dq = dq_s[...].T * (HEAD_DIM**-0.5)
        dq_ref[...] = dq.astype(BF)
        sum_ref[...] = jnp.sum(dq, axis=0, keepdims=True)


def backward_attention(q, g, ft, log, seg_row, k, v, mark):
    n_q, n_k = q.shape[0], k.shape[0]
    block = 512
    whole = lambda i: (0, 0)
    part = lambda i: (i, 0)
    return pl.pallas_call(
        backward_kernel,
        name="attention_backward",
        grid=(n_k // block,),
        in_specs=[
            pl.BlockSpec((n_q, GW), whole),
            pl.BlockSpec((n_q, GW), whole),
            pl.BlockSpec((GW, n_q), whole),
            pl.BlockSpec((GH, 1, n_q), lambda i: (0, 0, 0)),
            pl.BlockSpec((1, n_q), whole),
            pl.BlockSpec((block, GW), part),
            pl.BlockSpec((block, GW), part),
            pl.BlockSpec((block, HEAD_DIM), part),
        ],
        out_specs=[
            pl.BlockSpec((n_q, GW), whole),
            pl.BlockSpec((block, GW), part),
            pl.BlockSpec((block, GW), part),
            pl.BlockSpec((1, GW), whole),
        ],
        out_shape=[
            jax.ShapeDtypeStruct((n_q, GW), BF),
            jax.ShapeDtypeStruct((n_k, GW), BF),
            jax.ShapeDtypeStruct((n_k, GW), BF),
            jax.ShapeDtypeStruct((1, GW), F32),
        ],
        scratch_shapes=[
            pltpu.VMEM((GH, 2 * HEAD_DIM, n_q), BF),
            pltpu.VMEM((GH, 2 * HEAD_DIM, n_q), BF),
            pltpu.VMEM((GW, n_q), F32),
        ],
        compiler_params=pltpu.CompilerParams(vmem_limit_bytes=30 * 1024 * 1024),
        cost_estimate=pl.CostEstimate(
            flops=10 * n_q * n_k * 256 * GH, bytes_accessed=12 << 20, transcendentals=GH * n_q * n_k
        ),
    )(q, g, ft, log, seg_row, k, v, mark)


def body(
    tokens,
    segments,
    cotangent,
    ln1_gain,
    ln1_bias,
    qkv_weight,
    q_bias,
    v_bias,
    out_weight,
    out_bias,
    ln2_gain,
    ln2_bias,
    up_weight,
    up_bias,
    down_weight,
    down_bias,
):
    n_ctx, n_f = lax.axis_size("ctx"), lax.axis_size("fsdp")
    ring = n_ctx // GROUPS
    rows = tokens.shape[1]
    ctx, xi = lax.axis_index("ctx"), lax.axis_index("fsdp")
    zi, core = ctx // ring, ctx % 2
    f_masks = [1 << b for b in range(n_f.bit_length() - 1)]
    y_masks = [1 << b for b in range(1, ring.bit_length() - 1)]
    z_masks = [ring, 2 * ring]
    r_masks = y_masks + [1]
    f_order = orders(f_masks)

    all_seg = lax.all_gather(segments, "ctx", axis=1, tiled=True)[0]
    sent = tokens[0]
    z_blocks = [sent] + [swap(sent, "ctx", k * ring) for k in range(1, GROUPS)]
    row_tokens = jnp.concatenate(z_blocks, axis=0)

    def segs_of(distance):
        return lax.dynamic_slice_in_dim(all_seg, (ctx ^ distance) * rows, rows)

    own_cols = jnp.concatenate(
        [lax.dynamic_slice_in_dim(qkv_weight, p * D + zi * GW, GW, axis=1) for p in range(3)],
        axis=1,
    )
    small = jnp.concatenate(
        [ln1_gain, ln1_bias, q_bias, v_bias, out_bias, ln2_gain, ln2_bias, down_bias, up_bias]
    )
    small = jnp.pad(small.reshape(-1, 3 * GW), ((0, 16 - 16 // n_f), (0, 0)))
    first = jnp.concatenate([own_cols, small], axis=0)[None]
    first = lax.all_gather(first[0], "fsdp")
    share = D // n_f
    w_own = first[:, :share].reshape(D, 3 * GW)
    vectors = first[:, share : share + 16 // n_f].reshape(n_f, -1)

    def vector(i, width=share):
        return vectors[:, i * share : i * share + width].reshape(-1).astype(F32)

    gain_one, shift_one, bias_query, bias_value = (vector(i) for i in range(4))
    bias_out, gain_two, shift_two, bias_down = (vector(i) for i in range(4, 8))
    bias_up = vector(8, FF // n_f)

    wide = FF // n_f // 2
    w_out = lax.all_gather(out_weight, "fsdp", axis=0, tiled=True)
    up_sent = lax.dynamic_index_in_dim(
        up_weight.reshape(share, n_f, 2, wide), core, 2, keepdims=False
    ).reshape(share, n_f * wide)
    w_up = lax.all_gather(up_sent, "fsdp", axis=0, tiled=True)
    down_sent = lax.dynamic_slice_in_dim(down_weight, core * wide, wide, axis=0)
    w_down = lax.all_gather(down_sent, "fsdp", axis=0, tiled=True)
    w_qkv = lax.all_gather(qkv_weight, "fsdp", axis=0, tiled=True)
    bias_up = lax.dynamic_index_in_dim(bias_up.reshape(n_f, 2, wide), core, 1, False).reshape(-1)

    cot = cotangent[0]
    cot_both = gather(cot[None], "ctx", [1])

    unit_row, _ = standard(row_tokens.astype(F32))
    normed = (unit_row * gain_one + shift_one).astype(BF)
    qkv_f = jnp.dot(normed, w_own, preferred_element_type=F32)
    bq = lax.dynamic_slice_in_dim(bias_query, zi * GW, GW)
    bv = lax.dynamic_slice_in_dim(bias_value, zi * GW, GW)
    q = ((qkv_f[:, :GW] + bq) * (HEAD_DIM**-0.5 * LOG2E)).astype(BF)
    kv = jnp.concatenate([qkv_f[:, GW : 2 * GW], qkv_f[:, 2 * GW :] + bv], axis=1).astype(BF)
    kv_all = gather(kv[None], "ctx", r_masks)
    n_row = GROUPS * rows
    key_seg = jnp.concatenate(
        [segs_of(r ^ (k * ring)) for r in orders(r_masks) for k in range(GROUPS)]
    )
    row_seg = jnp.concatenate([segs_of(k * ring) for k in range(GROUPS)])
    keys = kv_all[:, :, :GW].reshape(-1, GW)
    values = kv_all[:, :, GW:].reshape(-1, GW)
    lane = lax.broadcasted_iota(jnp.int32, (1, HEAD_DIM), 1)
    mark = jnp.where(lane < 8, (key_seg[:, None] == lane), lane < 11).astype(BF)
    seg_row = row_seg.astype(F32)[None]

    attn_ft, attn_row, log_total = forward_attention(q, keys, values, mark, seg_row)

    attn_blocks = attn_row.reshape(GROUPS, rows, GW)
    got = jnp.stack([attn_blocks[0]] + [swap(attn_blocks[k], "ctx", k * ring) for k in range(1, GROUPS)])
    attn = arranged(got, list(range(GROUPS)), zi)
    attn = jnp.swapaxes(attn, 0, 1).reshape(rows, D)

    layer_in = tokens[0].astype(F32)
    mid = layer_in + jnp.dot(attn, w_out, preferred_element_type=F32) + bias_out
    unit_two, scale_two = standard(mid)
    normed_two = (unit_two * gain_two + shift_two).astype(BF)

    both = gather(normed_two[None], "ctx", [1]).reshape(2 * rows, D)
    up_pre = jnp.dot(both, w_up, preferred_element_type=F32) + bias_up
    hidden_f, gelu_back = jax.vjp(gelu_tanh, up_pre)
    hidden = hidden_f.astype(BF)
    cot_flat = cot_both.reshape(2 * rows, D)
    d_up = gelu_back(cols_product(cot_flat, w_down))[0]
    d_up_low = d_up.astype(BF)
    d_normed_part = cols_product(d_up_low, w_up)
    d_normed_two = d_normed_part[:rows] + swap(d_normed_part[rows:].astype(BF), "ctx", 1).astype(F32)
    out_part = jnp.dot(hidden, w_down, preferred_element_type=F32)
    out_stream = (
        mid + out_part[:rows] + swap(out_part[rows:].astype(BF), "ctx", 1).astype(F32) + bias_down
    )

    grad_stream = cot.astype(F32)
    d_gain_two = jnp.sum(d_normed_two * unit_two, axis=0)
    d_shift_two = jnp.sum(d_normed_two, axis=0)
    d_mid = grad_stream + standard_back(d_normed_two * gain_two, unit_two, scale_two)
    d_mid_low = d_mid.astype(BF)
    g_attn = cols_product(d_mid_low, w_out).astype(BF)
    g_blocks = arranged(jnp.swapaxes(g_attn.reshape(rows, GROUPS, GW), 0, 1), list(range(GROUPS)), zi)
    g_row = jnp.stack([g_blocks[0]] + [swap(g_blocks[k], "ctx", k * ring) for k in range(1, GROUPS)])
    g_row = g_row.reshape(n_row, GW)

    d_down_w = rows_product(hidden, cot_flat).astype(BF).reshape(n_f, wide, D)
    d_up_w = rows_product(both, d_up_low).astype(BF)
    d_up_w = jnp.concatenate(
        [d_up_w[:, j * wide : (j + 1) * wide].reshape(n_f, share, wide) for j in range(n_f)], axis=1
    )
    d_out_w = rows_product(attn, d_mid_low).astype(BF)
    same_core = [[i for i in range(n_ctx) if i % 2 == c] for c in range(2)]
    pairs = [[i, i + 1] for i in range(0, n_ctx, 2)]

    def summed(part, groups):
        part = lax.psum_scatter(part, "fsdp", scatter_dimension=0, tiled=False)
        return lax.psum(part, "ctx", axis_index_groups=groups)

    g_out_w = summed(d_out_w.reshape(n_f, share, D), None).astype(F32)
    g_down_w = lax.all_gather(summed(d_down_w, same_core), "ctx", axis_index_groups=pairs)
    g_down_w = g_down_w.reshape(-1, D).astype(F32)
    g_up_w = lax.all_gather(summed(d_up_w, same_core), "ctx", axis_index_groups=pairs)
    g_up_w = jnp.concatenate(
        [g_up_w[c, j * share : (j + 1) * share] for j in range(n_f) for c in range(2)], axis=1
    ).astype(F32)

    valid = (segments[0] > 0).astype(F32)[:, None]
    counts = jnp.stack(
        [
            jnp.sum(valid * layer_in * layer_in),
            jnp.sum(valid * mid * mid),
            jnp.sum(valid * out_stream * out_stream),
            jnp.sum(valid),
        ]
    )
    d_up_bias = jnp.sum(d_up, axis=0).reshape(n_f, 1, wide)
    d_up_bias = jnp.where(
        lax.broadcasted_iota(jnp.int32, (1, 2, 1), 1) == core, d_up_bias, 0.0
    ).reshape(-1, D)
    sums = jnp.concatenate(
        [
            jnp.stack(
                [
                    d_gain_two,
                    d_shift_two,
                    jnp.sum(d_mid, axis=0),
                    jnp.sum(grad_stream, axis=0),
                    jnp.pad(counts, (0, D - 4)),
                ]
            ),
            d_up_bias,
        ],
        axis=0,
    )
    d_q, d_k, d_v, d_bias_q = backward_attention(
        q, g_row, attn_ft, log_total, seg_row, keys, values, mark
    )
    d_kv = jnp.concatenate([d_k, d_v], axis=1).reshape(-1, n_row, 2 * GW)
    d_kv = reduce_blocks(d_kv, "ctx", r_masks)[0]
    d_bias_v = jnp.sum(d_kv[:, GW:].astype(F32), axis=0)
    d_qkv = jnp.concatenate([d_q, d_kv], axis=1)

    d_blocks = d_qkv.reshape(GROUPS, rows, 3 * GW)
    d_got = jnp.stack([d_blocks[0]] + [swap(d_blocks[k], "ctx", k * ring) for k in range(1, GROUPS)])
    d_got = arranged(d_got, list(range(GROUPS)), zi)
    d_own = jnp.concatenate(
        [d_got[g][:, p * GW : (p + 1) * GW] for p in range(3) for g in range(GROUPS)], axis=1
    )
    d_normed = cols_product(d_own, w_qkv)
    unit_one, scale_one = standard(layer_in)
    d_in = d_mid + standard_back(d_normed * gain_one, unit_one, scale_one)

    d_own_w = rows_product(normed, d_qkv).astype(BF)
    d_normed_row = cols_product(d_qkv, w_own)
    wide_q = jnp.zeros((GROUPS, GW), F32)
    group = lax.broadcasted_iota(jnp.int32, (GROUPS, 1), 0) == zi
    last = jnp.stack(
        [
            jnp.sum(d_normed_row * unit_row, axis=0),
            jnp.sum(d_normed_row, axis=0),
            jnp.where(group, d_bias_q, wide_q).reshape(-1),
            jnp.where(group, d_bias_v[None], wide_q).reshape(-1),
        ]
    )
    both_sums = lax.psum(jnp.concatenate([sums, last]), ("ctx", "fsdp"))
    sums, last = both_sums[: sums.shape[0]], both_sums[sums.shape[0] :]
    same_group = [[g * ring + r for r in range(ring)] for g in range(GROUPS)]
    same_place = [[g * ring + r for g in range(GROUPS)] for r in range(ring)]
    pieces = summed(d_own_w.reshape(n_f, share, 3 * GW), same_group)
    pieces = lax.all_gather(pieces, "ctx", axis_index_groups=same_place)
    g_qkv_w = jnp.concatenate(
        [pieces[g, :, q * GW : (q + 1) * GW] for q in range(3) for g in range(GROUPS)], axis=1
    ).astype(F32)

    def own(vec):
        return lax.dynamic_index_in_dim(vec.reshape(n_f, -1), xi, 0, keepdims=False)

    totals = sums[4, :4]
    return (
        out_stream.astype(BF)[None],
        d_in.astype(BF)[None],
        own(last[0]),
        own(last[1]),
        g_qkv_w,
        own(last[2]),
        own(last[3]),
        g_out_w,
        own(sums[2]),
        own(sums[0]),
        own(sums[1]),
        g_up_w,
        own(sums[5:]),
        g_down_w,
        own(sums[3]),
        jnp.sqrt(totals[:3] / (totals[3] * D)),
    )


def solution(mesh):
    token, vec, mat = P("fsdp", "ctx", None), P("fsdp"), P("fsdp", None)
    return jax.shard_map(
        body,
        mesh=mesh,
        in_specs=(
            token, P("fsdp", "ctx"), token, vec, vec, mat, vec, vec, mat, vec, vec, vec, mat, vec,
            mat, vec,
        ),
        out_specs=(
            token, token, vec, vec, mat, vec, vec, mat, vec, vec, vec, mat, vec, mat, vec, P(),
        ),
        check_vma=False,
    )
```

time: 1300 us -> 814 us (0.63)
  matrix products: 225 us -> 41.1 us
  other arithmetic: 199 us -> 46.6 us
  blocking collectives: 172 us -> 84.8 us
  local copies, waits for them, and re-layouts: 155 us -> 90.4 us
  waiting for transfers between devices: 518 us -> 455 us
  Pallas kernels: 0 us -> 52.6 us
  starting transfers between devices: 5.11 us -> 21.6 us
    psum x1 -> x3, waiting for transfers between devices: 15.3 us -> 235 us  [summed(): return lax.psum(part, 'ctx', axis_index_groups=groups)]
    ppermute x62 -> x20, waiting for transfers between devices: 240 us -> 56 us  [swap(): return lax.ppermute(block, axis, [(i, i ^ mask) for i in range(size)])]
    dot_general x116 -> x4, matrix products: 194 us -> 12.1 us  [the longest x1 5.06 us: body(): up_pre = jnp.dot(both, w_up, preferred_element_type=F32) + bias_up]
    dynamic_slice x80 -> x18, local copies, waits for them, and re-layouts: 99.3 us -> 13.6 us  [the longest x9 5.41 us: own(): return lax.dynamic_index_in_dim(vec.reshape(n_f, -1), xi, 0, keepdims=False)]
    convert_element_type x86 -> x10, other arithmetic: 90.1 us -> 15.6 us  [the longest x1 4.21 us: body(): g_down_w = g_down_w.reshape(-1, D).astype(F32)]
    psum x2 -> x1, blocking collectives: 100 us -> 41.5 us  [body(): both_sums = lax.psum(jnp.concatenate([sums, last]), ('ctx', 'fsdp'))]
    pallas_call x0 -> x2, Pallas kernels: none -> 52.6 us  [the longest x1 32.6 us: backward_attention(): pl.pallas_call(backward_kernel, name='attention_backward', grid=(n_k // b...]
    reduce_scatter x4, waiting for transfers between devices: 157 us -> 105 us  [summed(): part = lax.psum_scatter(part, 'fsdp', scatter_dimension=0, tiled=False)]
  transfers between devices with their start and end apart: 73 -> 34, of which waited for: 69 -> 16; matrix products, arithmetic and copies ran while one was open for 41% -> 17% of each run, Pallas kernels for 0% -> 2%
where the time goes in v1:
time: 814 us; the launch traced here: 809 us
  waiting for transfers between devices  455 us (56%)
  local copies, waits for them, and re-layouts  90.4 us (11%)
  blocking collectives  84.8 us (10%)
  Pallas kernels  52.6 us (6%)
  other arithmetic  46.6 us (6%)
  matrix products  41.1 us (5%)
  starting transfers between devices  21.6 us (3%)
  between operations  16.3 us (2%)
    psum x3, waiting for transfers between devices, summed(): return lax.psum(part, 'ctx', axis_index_groups=groups)  235 us
    reduce_scatter x4, waiting for transfers between devices, summed(): part = lax.psum_scatter(part, 'fsdp', scatter_dimension=0, tiled=False)  105 us
    ppermute x20, waiting for transfers between devices, swap(): return lax.ppermute(block, axis, [(i, i ^ mask) for i in range(size)])  56 us
    all_gather x1, waiting for transfers between devices, body(): w_qkv = lax.all_gather(qkv_weight, 'fsdp', axis=0, tiled=True)  45.5 us
    unnamed x213, local copies, waits for them, and re-layouts  42.6 us
    psum x1, blocking collectives, body(): both_sums = lax.psum(jnp.concatenate([sums, last]), ('ctx', 'fsdp'))  41.5 us
    pallas_call x1, Pallas kernels, backward_attention(): pl.pallas_call(backward_kernel, name='attention_backward', grid=(n_k // b...  32.6 us
    all_gather x1, blocking collectives, body(): all_seg = lax.all_gather(segments, 'ctx', axis=1, tiled=True)[0]  21.7 us
  transfers between devices with their start and end apart: 34, of which 16 were waited for; matrix products, arithmetic and copies ran while one was open for 17% of the time, Pallas kernels for 2%

profile of v1, /device:TPU:0, one launch (start us, length us, event | category | flops | bytes accessed | tf_op | source)
XLA Modules:
  0.0 808.6 jit_solution(3853213756940334481)
XLA Ops:
  8.0 3.1 collective-permute-start
  11.1 2.6 collective-permute-start.1
  13.7 4.3 copy.58
  18.0 2.6 constant_dynamic-slice_fusion.11
  24.2 21.6 %all-gather = bf16[800,576]{1,0:T(8,128)(2,1)S(1)} all-gather(bf16[400,576]{1,0:T(8,128)(2,1)S(1)} %fusion.42), channel_id=2, replica_groups=mesh['ctx'=16,'fsdp'=2] {'fsdp'}, dimensions={0}, use_global_device_ids=true | all-gather | bytes 1382400 | tf_op jit(solution)/shard_map/all_gather | solution.py:320
  52.5 21.7 %all_gather.37 = s32[1,4096]{1,0:T(1,128)S(1)} all-gather(s32[1,256]{1,0:T(1,128)} %param.20), channel_id=1, replica_groups=mesh['ctx'=16,'fsdp'=2] {'ctx'}, dimensions={1}, use_global_device_ids=true | all-gather | bytes 17408 | tf_op jit(solution)/shard_map/all_gather | solution.py:303
  84.3 1.6 fusion.7
  85.9 3.1 fusion.83
  90.5 19.6 %collective-permute-done.3 = bf16[1,1024,384]{1,2,0:T(8,128)(2,1)S(1)} collective-permute-done((bf16[1,1024,384]{1,2,0:T(8,128)(2,1)S(1)}, bf16[1,1024,384]{1,2,0:T(8,128)(2,1)S(1)}, u32[]{:S(2)}, u32[]{:S(2)}) %collective-permute-start.3) | collective-permute-done | bytes 786464 | tf_op jit(solution)/shard_map/ppermute | solution.py:26
  111.9 1.9 fusion.16.refs_3_.mark_ref
  113.8 2.4 copy.63
  116.2 2.1 multiply_convert_fusion.1.refs_0_.q_ref
  118.3 2.0 pad_maximum_fusion
  120.3 2.0 fusion.92
  122.3 3.7 copy.55
  126.1 3.7 copy.56
  129.8 1.6 copy-done.2
  131.4 1.6 copy-done.4
  134.0 20.0 %attention_forward.1 = (f32[192,1024]{1,0:T(8,128)S(1)}, bf16[1024,192]{1,0:T(8,128)(2,1)S(1)}, f32[3,1,1024]{2,1,0:T(1,128)S(1)}) custom-call(bf16[1024,192]{1,0:T(8,128)(2,1)S(1)} %copy-done.9, bf16[4096,192]{1,0:T(8,128)(2,1)S(1)} %bitcast.180, bf16[4096,192]{1,0:T(8,128)(2,1)S(1)} %bitcast.182, bf16[4096,64]{1,0:T(8,128)(2,1)S(1)} %fusion.16.refs_3_.mark_ref, ...), custom_call_target="tpu_custom_call" | custom-call | flops 12884901888 | bytes 8388608 | tf_op jit(solution)/shard_map/attention_forward/pallas_call | solution.py:149
  155.1 4.4 collective-permute-start.7
  163.0 5.3 collective-permute-done.6
  169.9 2.0 fusion.98
  173.2 2.0 pad_maximum_fusion.11
  176.2 5.1 convolution_add_fusion
  181.3 11.9 %all-gather.13.cloned.1.call-done = bf16[1536,768]{1,0:T(8,128)(2,1)} async-done(((bf16[768,768]{1,0:T(8,128)(2,1)}), bf16[1536,768]{1,0:T(8,128)(2,1)}) %all-gather.13.cloned.1.call-update) | async-done | bytes 2359312 | tf_op jit(solution)/shard_map/all_gather | solution.py:339
  193.2 5.3 fusion.88
  202.3 1.9 fusion.85
  205.6 1.8 collective-permute-done.9
  207.4 3.5 multiply_reduce_fusion
  213.4 1.9 copy.59
  216.4 1.6 collective-permute-start.12
  218.0 2.4 collective-permute-start.13
  221.3 7.3 collective-permute-done.13
  229.5 2.0 copy.60
  231.5 1.6 copy-done.5
  236.3 32.6 %attention_backward.1 = (bf16[1024,192]{1,0:T(8,128)(2,1)S(1)}, bf16[4096,192]{1,0:T(8,128)(2,1)S(1)}, bf16[4096,192]{1,0:T(8,128)(2,1)S(1)}, f32[1,192]{1,0:T(1,128)S(1)}) custom-call(bf16[1024,192]{1,0:T(8,128)(2,1)S(1)} %copy-done.10, bf16[1024,192]{1,0:T(8,128)(2,1)S(1)} %bitcast.184, f32[192,1024]{1,0:T(8,128)S(1)} %copy-done.12, ...), custom_call_target="tpu_custom_call" | custom-call | flops 32212254720 | bytes 12582912 | tf_op jit(solution)/shard_map/attention_backward/pallas_call | solution.py:236
  270.1 3.4 collective-permute-done.15
  274.1 1.5 collective-permute-start.16
  275.7 18.1 %collective-permute-done.16 = bf16[1,1024,384]{2,1,0:T(8,128)(2,1)S(1)} collective-permute-done((bf16[1,1024,384]{2,1,0:T(8,128)(2,1)S(1)}, bf16[1,1024,384]{2,1,0:T(8,128)(2,1)S(1)}, u32[]{:S(2)}, u32[]{:S(2)}) %collective-permute-start.16) | collective-permute-done | bytes 786464 | tf_op jit(solution)/shard_map/ppermute | solution.py:26
  294.1 2.9 convolution_convert_fusion.3
  300.1 3.1 convolution_convert_fusion.1
  303.3 1.6 pad_maximum_fusion.1
  305.0 5.2 convolution_convert_fusion
  310.3 5.7 reduce-scatter.5.cloned.1.call-done
  316.0 24.4 %reduce-scatter.7.cloned.1.call-done = bf16[1,384,768]{2,1,0:T(8,128)(2,1)} async-done(((bf16[2,384,768]{2,1,0:T(8,128)(2,1)}), bf16[1,384,768]{2,1,0:T(8,128)(2,1)}) %reduce-scatter.7.cloned.1.call-update) | async-done | bytes 589840 | tf_op jit(solution)/shard_map/reduce_scatter | solution.py:411
  340.5 37.4 %reduce-scatter.9.cloned.1.call-done = bf16[1,768,768]{2,1,0:T(8,128)(2,1)} async-done(((bf16[2,768,768]{2,1,0:T(8,128)(2,1)}), bf16[1,768,768]{2,1,0:T(8,128)(2,1)}) %reduce-scatter.9.cloned.1.call-update) | async-done | bytes 1179664 | tf_op jit(solution)/shard_map/reduce_scatter | solution.py:411
  377.9 37.6 %reduce-scatter.11.cloned.1.call-done = bf16[1,768,768]{2,1,0:T(8,128)(2,1)} async-done(((bf16[2,768,768]{2,1,0:T(8,128)(2,1)}), bf16[1,768,768]{2,1,0:T(8,128)(2,1)}) %reduce-scatter.11.cloned.1.call-update) | async-done | bytes 1179664 | tf_op jit(solution)/shard_map/reduce_scatter | solution.py:411
  416.3 34.5 %all-reduce.7.cloned.1.call-done = bf16[1,384,576]{1,2,0:T(8,128)(2,1)} async-done(((bf16[1,384,576]{1,2,0:T(8,128)(2,1)}), bf16[1,384,576]{1,2,0:T(8,128)(2,1)}) %all-reduce.7.cloned.1.call-update) | async-done | bytes 442384 | tf_op jit(solution)/shard_map/psum | solution.py:412
  456.2 1.6 fusion.48
  459.3 2.4 collective-permute-start.18
  462.2 3.8 fusion.86
  466.0 92.8 %all-reduce.9.cloned.1.call-done = bf16[384,768]{1,0:T(8,128)(2,1)} async-done(((bf16[384,768]{1,0:T(8,128)(2,1)}), bf16[384,768]{1,0:T(8,128)(2,1)}) %all-reduce.9.cloned.1.call-update) | async-done | bytes 589840 | tf_op jit(solution)/shard_map/psum | solution.py:412
  558.8 2.2 convert_element_type.268
  562.6 107.7 %all-reduce.11.cloned.1.call-done = (bf16[1,768,768]{2,1,0:T(8,128)(2,1)}, bf16[1,768,768]{2,1,0:T(8,128)(2,1)}) async-done(((bf16[1,768,768]{2,1,0:T(8,128)(2,1)}, bf16[1,768,768]{2,1,0:T(8,128)(2,1)}), (bf16[1,768,768]{2,1,0:T(8,128)(2,1)}, bf16[1,768,768]{2,1,0:T(8,128)(2,1)})) %all-reduce.11.cloned.1.call-update) | async-done | bytes 2359312 | tf_op jit(solution)/shard_map/psum | solution.py:412
  672.3 2.5 concatenate.89
  674.9 45.5 %all-gather.15.cloned.1.call-done = bf16[768,2304]{1,0:T(8,128)(2,1)} async-done(((bf16[384,2304]{1,0:T(8,128)(2,1)}), bf16[768,2304]{1,0:T(8,128)(2,1)}) %all-gather.15.cloned.1.call-update) | async-done | bytes 3538960 | tf_op jit(solution)/shard_map/all_gather | solution.py:340
  720.4 4.6 fusion.87
  725.0 2.7 select_maximum_fusion
  727.9 41.5 %psum.35 = f32[13,768]{1,0:T(8,128)S(1)} all-reduce(f32[13,768]{1,0:T(8,128)S(1)} %concatenate.90), channel_id=1, replica_groups=mesh['ctx'=16,'fsdp'=2] {'ctx','fsdp'}, use_global_device_ids=true, to_apply=%region_22.23 | all-reduce | flops 9984 | bytes 79872 | tf_op jit(solution)/shard_map/psum | solution.py:480
  776.8 2.2 fusion.46
  790.4 2.7 copy.62
  793.1 1.8 slice_bitcast_fusion.3
  794.9 2.8 maximum_convert_fusion
  797.7 4.2 bitcast_convert_fusion
  (387 shorter events, 82.2 us)
Async XLA Ops:
  7.2 152.3 %copy-start = (bf16[1536,768]{1,0:T(8,128)(2,1)S(1)}, bf16[1536,768]{1,0:T(8,128)(2,1)}, u32[]{:S(2)}) copy-start(bf16[1536,768]{1,0:T(8,128)(2,1)} %param.33) | copy-start | bytes 7077892
  7.2 162.7 %all-gather.9.cloned.1.call-start = ((), (), s32[]{:S(2)}) async-start(), calls=%async_computation.4 | async-start | bytes 1769472 | tf_op jit(solution)/shard_map/all_gather | solution.py:333
  7.9 168.3 %all-gather.11.cloned.1.call-start = ((), (), s32[]{:S(2)}) async-start(), calls=%async_computation.5 | async-start | bytes 3538944 | tf_op jit(solution)/shard_map/all_gather | solution.py:337
  8.0 74.7 %collective-permute-start = (bf16[256,768]{1,0:T(8,128)(2,1)}, bf16[256,768]{1,0:T(8,128)(2,1)S(1)}, u32[]{:S(2)}, u32[]{:S(2)}) collective-permute-start(bf16[256,768]{1,0:T(8,128)(2,1)} %bitcast.186), channel_id=1, source_target_pairs={{0,8},{2,10},{4,12},{6,14},{8,0},{10,2},{12,4},{14,6},{16,24},{18,... | collective-permute-start | bytes 1179656 | tf_op jit(solution)/shard_map/ppermute | solution.py:26
  11.1 71.6 %collective-permute-start.1 = (bf16[256,768]{1,0:T(8,128)(2,1)}, bf16[256,768]{1,0:T(8,128)(2,1)S(1)}, u32[]{:S(2)}, u32[]{:S(2)}) collective-permute-start(bf16[256,768]{1,0:T(8,128)(2,1)} %bitcast.187), channel_id=1, source_target_pairs={{0,16},{2,18},{4,20},{6,22},{8,24},{10,26},{12,28},{14,30},{16,0},... | collective-permute-start | bytes 1179656 | tf_op jit(solution)/shard_map/ppermute | solution.py:26
  13.7 69.1 %collective-permute-start.2 = (bf16[256,768]{1,0:T(8,128)(2,1)}, bf16[256,768]{1,0:T(8,128)(2,1)}, u32[]{:S(2)}, u32[]{:S(2)}) collective-permute-start(bf16[256,768]{1,0:T(8,128)(2,1)} %bitcast.188), channel_id=1, source_target_pairs={{0,24},{2,26},{4,28},{6,30},{8,16},{10,18},{12,20},{14,22},{16,8},... | collective-permute-start | bytes 1179656 | tf_op jit(solution)/shard_map/ppermute | solution.py:26
  13.7 159.6 %collective-permute-start.10 = (bf16[1,256,768]{2,1,0:T(8,128)(2,1)}, bf16[1,256,768]{2,1,0:T(8,128)(2,1)}, u32[]{:S(2)}, u32[]{:S(2)}) collective-permute-start(bf16[1,256,768]{2,1,0:T(8,128)(2,1)} %param.21), channel_id=1, source_target_pairs={{0,2},{2,0},{4,6},{6,4},{8,10},{10,8},{12,14},{14,12},{16,18},{18,... | collective-permute-start | bytes 1179656 | tf_op jit(solution)/shard_map/ppermute | solution.py:26
  20.6 172.6 %all-gather.13.cloned.1.call-start = ((), (), s32[]{:S(2)}) async-start(), calls=%async_computation.6 | async-start | bytes 3538944 | tf_op jit(solution)/shard_map/all_gather | solution.py:339
  24.0 58.7 %copy-start.13 = (bf16[1,256,768]{2,1,0:T(8,128)(2,1)S(1)}, bf16[1,256,768]{2,1,0:T(8,128)(2,1)}, u32[]{:S(2)}) copy-start(bf16[1,256,768]{2,1,0:T(8,128)(2,1)} %param.19) | copy-start | bytes 1179652
  89.2 21.0 %copy-start.18 = (bf16[1,1024,192]{1,2,0:T(8,128)(2,1)}, bf16[1,1024,192]{1,2,0:T(8,128)(2,1)S(1)}, u32[]{:S(2)}) copy-start(bf16[1,1024,192]{1,2,0:T(8,128)(2,1)S(1)} %fusion.44) | copy-start | bytes 1179652
  90.2 21.4 %copy-start.19 = (bf16[1,1024,192]{1,2,0:T(8,128)(2,1)}, bf16[1,1024,192]{1,2,0:T(8,128)(2,1)S(1)}, u32[]{:S(2)}) copy-start(bf16[1,1024,192]{1,2,0:T(8,128)(2,1)S(1)} %get-tuple-element.84) | copy-start | bytes 1179652
  90.2 21.5 %copy-start.48 = (f32[2,384]{1,0:T(2,128)S(1)}, f32[2,384]{1,0:T(2,128)}, u32[]{:S(2)}) copy-start(f32[2,384]{1,0:T(2,128)} %get-tuple-element.126) | copy-start | bytes 9220
  90.2 21.6 %copy-start.68 = (s32[1,256]{1,0:T(1,128)S(1)}, s32[1,256]{1,0:T(1,128)}, u32[]{:S(2)}) copy-start(s32[1,256]{1,0:T(1,128)} %get-tuple-element.130) | copy-start | bytes 3076
  90.2 21.6 %copy-start.67 = (s32[1,256]{1,0:T(1,128)S(1)}, s32[1,256]{1,0:T(1,128)}, u32[]{:S(2)}) copy-start(s32[1,256]{1,0:T(1,128)} %get-tuple-element.129) | copy-start | bytes 3076
  90.2 21.6 %copy-start.52 = (s32[1,256]{1,0:T(1,128)S(1)}, s32[1,256]{1,0:T(1,128)}, u32[]{:S(2)}) copy-start(s32[1,256]{1,0:T(1,128)} %copy-done.51) | copy-start | bytes 3076
  90.2 21.6 %copy-start.54 = (s32[1,256]{1,0:T(1,128)S(1)}, s32[1,256]{1,0:T(1,128)}, u32[]{:S(2)}) copy-start(s32[1,256]{1,0:T(1,128)} %copy-done.53) | copy-start | bytes 3076
  90.2 21.6 %copy-start.56 = (s32[1,256]{1,0:T(1,128)S(1)}, s32[1,256]{1,0:T(1,128)}, u32[]{:S(2)}) copy-start(s32[1,256]{1,0:T(1,128)} %copy-done.55) | copy-start | bytes 3076
  90.2 21.6 %copy-start.58 = (s32[1,256]{1,0:T(1,128)S(1)}, s32[1,256]{1,0:T(1,128)}, u32[]{:S(2)}) copy-start(s32[1,256]{1,0:T(1,128)} %copy-done.57) | copy-start | bytes 3076
  90.2 21.6 %copy-start.82 = (pred[64]{0:T(512)(128)(4,1)S(1)}, pred[64]{0:T(512)(128)(4,1)}, u32[]{:S(2)}) copy-start(pred[64]{0:T(512)(128)(4,1)} %get-tuple-element.150) | copy-start | bytes 196
  90.3 21.6 %copy-start.83 = (pred[64]{0:T(512)(128)(4,1)S(1)}, pred[64]{0:T(512)(128)(4,1)}, u32[]{:S(2)}) copy-start(pred[64]{0:T(512)(128)(4,1)} %get-tuple-element.151) | copy-start | bytes 196
  90.3 19.8 %collective-permute-start.3 = (bf16[1,1024,384]{1,2,0:T(8,128)(2,1)S(1)}, bf16[1,1024,384]{1,2,0:T(8,128)(2,1)S(1)}, u32[]{:S(2)}, u32[]{:S(2)}) collective-permute-start(bf16[1,1024,384]{1,2,0:T(8,128)(2,1)S(1)} %pad_maximum_fusion.9), channel_id=1, source_target_pairs={{0,4},{2,6},{4,0},{6,2},{8,12},{10,14},{12,8},{14,10},{16,20},{18,... | collective-permute-start | bytes 2359304 | tf_op jit(solution)/shard_map/ppermute | solution.py:26
  111.5 6.8 collective-permute-start.4
  155.1 7.9 collective-permute-start.5
  155.1 13.2 %collective-permute-start.6 = (bf16[256,192]{1,0:T(8,128)(2,1)}, bf16[256,192]{1,0:T(8,128)(2,1)}, u32[]{:S(2)}, u32[]{:S(2)}) collective-permute-start(bf16[256,192]{1,0:T(8,128)(2,1)} %get-tuple-element.103), channel_id=1, source_target_pairs={{0,16},{2,18},{4,20},{6,22},{8,24},{10,26},{12,28},{14,30},{16,0},... | collective-permute-start | bytes 294920 | tf_op jit(solution)/shard_map/ppermute | solution.py:26
  155.1 13.2 %collective-permute-start.7 = (bf16[256,192]{1,0:T(8,128)(2,1)}, bf16[256,192]{1,0:T(8,128)(2,1)}, u32[]{:S(2)}, u32[]{:S(2)}) collective-permute-start(bf16[256,192]{1,0:T(8,128)(2,1)} %get-tuple-element.102), channel_id=1, source_target_pairs={{0,24},{2,26},{4,28},{6,30},{8,16},{10,18},{12,20},{14,22},{16,8},... | collective-permute-start | bytes 294920 | tf_op jit(solution)/shard_map/ppermute | solution.py:26
  160.7 155.3 %reduce-scatter.5.cloned.1.call-start = ((), (), s32[]{:S(2)}) async-start(), calls=%async_computation.8 | async-start | bytes 1327104 | tf_op jit(solution)/shard_map/reduce_scatter | solution.py:411
  172.4 2.9 collective-permute-start.8
  201.2 4.4 collective-permute-start.11
  205.4 1.9 collective-permute-start.9
  216.4 4.9 collective-permute-start.12
  218.0 10.7 %collective-permute-start.13 = (bf16[256,192]{0,1:T(8,128)(2,1)S(1)}, bf16[256,192]{0,1:T(8,128)(2,1)S(1)}, u32[]{:S(2)}, u32[]{:S(2)}) collective-permute-start(bf16[256,192]{0,1:T(8,128)(2,1)S(1)} %get-tuple-element.107), channel_id=1, source_target_pairs={{0,16},{2,18},{4,20},{6,22},{8,24},{10,26},{12,28},{14,30},{16,0},... | collective-permute-start | bytes 294920 | tf_op jit(solution)/shard_map/ppermute | solution.py:26
  220.4 8.3 %collective-permute-start.14 = (bf16[256,192]{0,1:T(8,128)(2,1)S(1)}, bf16[256,192]{0,1:T(8,128)(2,1)S(1)}, u32[]{:S(2)}, u32[]{:S(2)}) collective-permute-start(bf16[256,192]{0,1:T(8,128)(2,1)S(1)} %get-tuple-element.106), channel_id=1, source_target_pairs={{0,24},{2,26},{4,28},{6,30},{8,16},{10,18},{12,20},{14,22},{16,8},... | collective-permute-start | bytes 294920 | tf_op jit(solution)/shard_map/ppermute | solution.py:26
  268.9 25.1 %copy-start.6 = (bf16[1024,192]{1,0:T(8,128)(2,1)}, bf16[1024,192]{1,0:T(8,128)(2,1)S(1)}, u32[]{:S(2)}) copy-start(bf16[1024,192]{1,0:T(8,128)(2,1)S(1)} %get-tuple-element.26) | copy-start | bytes 1179652
  270.1 3.5 collective-permute-start.15
  274.0 20.0 %copy-start.15 = (bf16[1,256,768]{2,1,0:T(8,128)(2,1)S(1)}, bf16[1,256,768]{2,1,0:T(8,128)(2,1)}, u32[]{:S(2)}) copy-start(bf16[1,256,768]{2,1,0:T(8,128)(2,1)} %param.19) | copy-start | bytes 1179652
  274.0 20.0 %copy-start.29 = (bf16[256,768]{1,0:T(8,128)(2,1)S(1)}, bf16[256,768]{1,0:T(8,128)(2,1)}, u32[]{:S(2)}) copy-start(bf16[256,768]{1,0:T(8,128)(2,1)} %copy-done.28) | copy-start | bytes 1179652
  274.0 20.0 %copy-start.31 = (bf16[256,768]{1,0:T(8,128)(2,1)S(1)}, bf16[256,768]{1,0:T(8,128)(2,1)}, u32[]{:S(2)}) copy-start(bf16[256,768]{1,0:T(8,128)(2,1)} %copy-done.30) | copy-start | bytes 1179652
  274.0 20.0 %copy-start.41 = (f32[1024]{0:T(1024)S(1)}, f32[1024]{0:T(1024)}, u32[]{:S(2)}) copy-start(f32[1024]{0:T(1024)} %copy-done.40) | copy-start | bytes 12292
  274.0 20.0 %copy-start.62 = (f32[768]{0:T(1024)S(1)}, f32[768]{0:T(1024)}, u32[]{:S(2)}) copy-start(f32[768]{0:T(1024)} %reshape.459) | copy-start | bytes 9220
  274.1 19.6 %collective-permute-start.16 = (bf16[1,1024,384]{2,1,0:T(8,128)(2,1)S(1)}, bf16[1,1024,384]{2,1,0:T(8,128)(2,1)S(1)}, u32[]{:S(2)}, u32[]{:S(2)}) collective-permute-start(bf16[1,1024,384]{2,1,0:T(8,128)(2,1)S(1)} %slice.358), channel_id=1, source_target_pairs={{0,4},{2,6},{4,0},{6,2},{8,12},{10,14},{12,8},{14,10},{16,20},{18,... | collective-permute-start | bytes 2359304 | tf_op jit(solution)/shard_map/ppermute | solution.py:26
  298.0 42.3 %reduce-scatter.7.cloned.1.call-start = ((), (), s32[]{:S(2)}) async-start(), calls=%async_computation.11 | async-start | bytes 1769472 | tf_op jit(solution)/shard_map/reduce_scatter | solution.py:411
  300.0 77.9 %reduce-scatter.9.cloned.1.call-start = ((), (), s32[]{:S(2)}) async-start(), calls=%async_computation.13 | async-start | bytes 3538944 | tf_op jit(solution)/shard_map/reduce_scatter | solution.py:411
  304.9 110.6 %reduce-scatter.11.cloned.1.call-start = ((), (), s32[]{:S(2)}) async-start(), calls=%async_computation.15 | async-start | bytes 3538944 | tf_op jit(solution)/shard_map/reduce_scatter | solution.py:411
  310.2 140.6 %all-reduce.7.cloned.1.call-start = ((), (), s32[]{:S(2)}) async-start(), calls=%async_computation.9 | async-start | bytes 884736 | tf_op jit(solution)/shard_map/psum | solution.py:412
  316.0 242.8 %all-reduce.9.cloned.1.call-start = ((), (), s32[]{:S(2)}) async-start(), calls=%async_computation.12 | async-start | bytes 1179648 | tf_op jit(solution)/shard_map/psum | solution.py:412
  340.4 110.5 %copy-start.24 = (bf16[1,256,768]{2,1,0:T(8,128)(2,1)S(1)}, bf16[1,256,768]{2,1,0:T(8,128)(2,1)}, u32[]{:S(2)}) copy-start(bf16[1,256,768]{2,1,0:T(8,128)(2,1)} %param.21) | copy-start | bytes 1179652
  340.4 329.9 %all-reduce.11.cloned.1.call-start = ((), (), s32[]{:S(2)}) async-start(), calls=%async_computation.17 | async-start | bytes 4718592 | tf_op jit(solution)/shard_map/psum | solution.py:412
  415.5 40.7 %copy-start.7 = (bf16[1024,192]{1,0:T(8,128)(2,1)S(1)}, bf16[1024,192]{1,0:T(8,128)(2,1)}, u32[]{:S(2)}) copy-start(bf16[1024,192]{1,0:T(8,128)(2,1)} %copy-done.6) | copy-start | bytes 1179652
  415.5 304.9 %all-gather.15.cloned.1.call-start = ((), (), s32[]{:S(2)}) async-start(), calls=%async_computation.7 | async-start | bytes 5308416 | tf_op jit(solution)/shard_map/all_gather | solution.py:340
  416.2 362.8 %all-gather.17.cloned.1.call-start = ((), (), s32[]{:S(2)}) async-start(), calls=%async_computation.10 | async-start | bytes 2211840 | tf_op jit(solution)/shard_map/all_gather | solution.py:485
  450.8 342.3 %all-gather.19.cloned.1.call-start = ((), (), s32[]{:S(2)}) async-start(), calls=%async_computation.14 | async-start | bytes 3538944 | tf_op jit(solution)/shard_map/all_gather | solution.py:417
  457.8 103.1 %collective-permute-start.17 = (bf16[256,576]{1,0:T(8,128)(2,1)}, bf16[256,576]{1,0:T(8,128)(2,1)}, u32[]{:S(2)}, u32[]{:S(2)}) collective-permute-start(bf16[256,576]{1,0:T(8,128)(2,1)} %get-tuple-element.94), channel_id=1, source_target_pairs={{0,8},{2,10},{4,12},{6,14},{8,0},{10,2},{12,4},{14,6},{16,24},{18,... | collective-permute-start | bytes 884744 | tf_op jit(solution)/shard_map/ppermute | solution.py:26
  459.3 101.6 %collective-permute-start.18 = (bf16[256,576]{1,0:T(8,128)(2,1)}, bf16[256,576]{1,0:T(8,128)(2,1)}, u32[]{:S(2)}, u32[]{:S(2)}) collective-permute-start(bf16[256,576]{1,0:T(8,128)(2,1)} %get-tuple-element.95), channel_id=1, source_target_pairs={{0,16},{2,18},{4,20},{6,22},{8,24},{10,26},{12,28},{14,30},{16,0},... | collective-permute-start | bytes 884744 | tf_op jit(solution)/shard_map/ppermute | solution.py:26
  461.7 99.2 %collective-permute-start.19 = (bf16[256,576]{1,0:T(8,128)(2,1)}, bf16[256,576]{1,0:T(8,128)(2,1)}, u32[]{:S(2)}, u32[]{:S(2)}) collective-permute-start(bf16[256,576]{1,0:T(8,128)(2,1)} %get-tuple-element.96), channel_id=1, source_target_pairs={{0,24},{2,26},{4,28},{6,30},{8,16},{10,18},{12,20},{14,22},{16,8},... | collective-permute-start | bytes 884744 | tf_op jit(solution)/shard_map/ppermute | solution.py:26
  670.4 127.3 %all-gather.21.cloned.1.call-start = ((), (), s32[]{:S(2)}) async-start(), calls=%async_computation.16 | async-start | bytes 3538944 | tf_op jit(solution)/shard_map/all_gather | solution.py:415
  670.6 49.8 %copy-start.50 = (f32[256]{0:T(256)S(1)}, f32[256]{0:T(256)}, u32[]{:S(2)}) copy-start(f32[256]{0:T(256)} %copy-done.49) | copy-start | bytes 3076
  670.6 49.8 %copy-start.60 = (f32[256]{0:T(256)S(1)}, f32[256]{0:T(256)}, u32[]{:S(2)}) copy-start(f32[256]{0:T(256)} %add_rsqrt_fusion.1) | copy-start | bytes 3076
  670.6 49.7 %copy-start.63 = (f32[768]{0:T(1024)S(1)}, f32[768]{0:T(1024)}, u32[]{:S(2)}) copy-start(f32[768]{0:T(1024)} %reshape.459) | copy-start | bytes 9220
  670.7 49.7 %copy-start.73 = (f32[1,256]{1,0:T(1,128)S(1)}, f32[1,256]{1,0:T(1,128)}, u32[]{:S(2)}) copy-start(f32[1,256]{1,0:T(1,128)} %copy-done.72) | copy-start | bytes 3076
  674.8 52.9 %copy-start.42 = (f32[1,768]{1,0:T(1,128)S(1)}, f32[1,768]{1,0:T(1,128)}, u32[]{:S(2)}) copy-start(f32[1,768]{1,0:T(1,128)} %stack.95) | copy-start | bytes 9220
  674.8 52.9 %copy-start.43 = (f32[1,768]{1,0:T(1,128)S(1)}, f32[1,768]{1,0:T(1,128)}, u32[]{:S(2)}) copy-start(f32[1,768]{1,0:T(1,128)} %stack.93) | copy-start | bytes 9220
  674.8 52.9 %copy-start.44 = (f32[1,768]{1,0:T(1,128)S(1)}, f32[1,768]{1,0:T(1,128)}, u32[]{:S(2)}) copy-start(f32[1,768]{1,0:T(1,128)} %stack.94) | copy-start | bytes 9220
  674.8 52.9 %copy-start.45 = (f32[1,768]{1,0:T(1,128)S(1)}, f32[1,768]{1,0:T(1,128)}, u32[]{:S(2)}) copy-start(f32[1,768]{1,0:T(1,128)} %select_n.235) | copy-start | bytes 9220
  674.9 52.9 %copy-start.46 = (f32[1,768]{1,0:T(1,128)S(1)}, f32[1,768]{1,0:T(1,128)}, u32[]{:S(2)}) copy-start(f32[1,768]{1,0:T(1,128)} %select_n.237) | copy-start | bytes 9220
  (58 other events, 312.7 us)
Sparse Core Ops, SparseCore 0:
  9.6 32.3 all-gather.8
  44.1 35.6 all-gather.10
  160.8 32.4 all-gather.12
  298.2 17.7 reduce-scatter.4
  318.6 21.7 reduce-scatter.6
  343.2 34.6 reduce-scatter.8
  380.7 34.7 reduce-scatter.10
  418.0 32.7 all-reduce.6
  454.1 104.5 all-reduce.8
  562.2 108.0 all-reduce.10
  672.0 48.3 all-gather.14
  721.9 41.3 all-gather.16
  764.9 9.8 all-gather.18
  779.1 11.4 all-gather.20
